TPU v7x, 128 devices: a whole 4x4x4 slice. The times are simulated.
128 devices in a mesh: section: 2 (over x_lo), dp: 8 (over x_hi, y), tensor: 8 (over z, core).
Axes of the slice: x: 4 (x_hi: 2, x_lo: 2; x = x_hi * 2 + x_lo), y: 4, z: 4, core: 2. Of those that a mesh axis runs over, the one named last changes fastest.
Arguments:
- tokens: bfloat16 [2048, 8192], P('dp', ('section', 'tensor')), may hold values from -6 to 6
- segment_ids: int32 [8, 256], P('dp'), may hold values from 0 to 3, never falling along the last dimension, each value on 1 to 128 neighbouring positions
- gain_attn: float32 [8192], replicated, may hold values from 0.1 to 1.9
- w_query: bfloat16 [8192, 4096], P(None, ('section', 'tensor')), may hold values from -0.06629126 to 0.06629126
- w_key: bfloat16 [8192, 4096], P(None, ('section', 'tensor')), may hold values from -0.06629126 to 0.06629126
- w_value: bfloat16 [8192, 4096], P(None, ('section', 'tensor')), may hold values from -0.0625 to 0.0625
- w_output: bfloat16 [4096, 8192], P(('section', 'tensor')), may hold values from -0.09375 to 0.09375
- gain_ffn: float32 [8192], replicated, may hold values from 0.1 to 1.9
- w_up: bfloat16 [8192, 16384], P(('section', 'tensor'), 'dp'), may hold values from -0.0625 to 0.0625
- w_down: bfloat16 [16384, 8192], P('dp', ('section', 'tensor')), may hold values from -0.046875 to 0.046875
Outputs:
- layer_out: bfloat16 [2048, 8192], P('dp', ('section', 'tensor'))
Inputs may be any that keep to these rules, and one draw needn't show every extreme that they name: `segment_ids`: segment numbers never fall along a replica's tokens; each segment holds 1 to 128 tokens.
All inputs are finite; a program needn't handle non-finite values.
Results may differ from a plain program's by a relative error of at most 0.023.
Values may be sent and summed in bfloat16 or wider, within the bound.
A program may use at most 128 MiB of HBM per device.

v0:
```python
import jax
import jax.numpy as jnp
from jax import lax
from jax.sharding import PartitionSpec as P

HD = 128


def layer_norm(values, gain):
    mean = jnp.mean(values, axis=-1, keepdims=True)
    second = jnp.mean(values * values, axis=-1, keepdims=True)
    return (values - mean) * lax.rsqrt(second - mean * mean + 1e-05) * gain


def per_device(
    tokens, segment_ids, gain_attn, w_query, w_key, w_value, w_output, gain_ffn, w_up, w_down
):
    tok_rows = tokens.shape[0]
    width = gain_attn.shape[0]
    groups = lax.axis_size(("section", "tensor"))
    share = width // groups
    first_col = lax.axis_index(("section", "tensor")) * share
    whole = lax.all_gather(tokens, ("section", "tensor"), axis=1, tiled=True)
    normed = layer_norm(whole.astype(jnp.float32), gain_attn).astype(jnp.bfloat16)
    local_heads = w_query.shape[1] // HD
    query = jnp.dot(normed, w_query, preferred_element_type=jnp.float32).astype(jnp.bfloat16)
    key = jnp.dot(normed, w_key, preferred_element_type=jnp.float32).astype(jnp.bfloat16)
    value = jnp.dot(normed, w_value, preferred_element_type=jnp.float32).astype(jnp.bfloat16)
    query = query.reshape(tok_rows, local_heads, HD)
    key = key.reshape(tok_rows, local_heads, HD)
    value = value.reshape(tok_rows, local_heads, HD)
    scores = jnp.einsum("qhd,khd->hqk", query, key, preferred_element_type=jnp.float32) * HD ** (
        -0.5
    )
    position = jnp.arange(tok_rows)
    segment_row = segment_ids[0]
    keep = jnp.logical_and(
        position[:, None] >= position[None, :], segment_row[:, None] == segment_row[None, :]
    )
    scores = jnp.where(keep[None], scores, -1e30)
    top = jnp.max(scores, axis=-1, keepdims=True)
    expo = jnp.exp(scores - top)
    probs = (expo / jnp.sum(expo, axis=-1, keepdims=True)).astype(jnp.bfloat16)
    context = jnp.einsum("hqk,khd->qhd", probs, value, preferred_element_type=jnp.float32)
    context = context.astype(jnp.bfloat16).reshape(tok_rows, local_heads * HD)
    partial_out = jnp.dot(context, w_output, preferred_element_type=jnp.float32)
    summed = lax.psum(partial_out.astype(jnp.bfloat16), ("section", "tensor")).astype(jnp.float32)
    resid_full = (whole.astype(jnp.float32) + summed).astype(jnp.bfloat16)
    normed_full = layer_norm(resid_full.astype(jnp.float32), gain_ffn).astype(jnp.bfloat16)
    normed_ffn = lax.dynamic_slice_in_dim(normed_full, first_col, share, 1)
    resid_mid = lax.dynamic_slice_in_dim(resid_full, first_col, share, 1)
    gathered = lax.all_gather(normed_ffn, "dp", axis=0, tiled=True)
    pre_act = lax.psum_scatter(
        jnp.dot(gathered, w_up, preferred_element_type=jnp.float32).astype(jnp.bfloat16),
        ("section", "tensor"),
        scatter_dimension=0,
        tiled=True,
    ).astype(jnp.float32)
    activated = jax.nn.gelu(pre_act, approximate=True).astype(jnp.bfloat16)
    partial_down = jnp.dot(
        lax.all_gather(activated, ("section", "tensor"), axis=0, tiled=True),
        w_down,
        preferred_element_type=jnp.float32,
    )
    ffn_out = lax.psum_scatter(
        partial_down.astype(jnp.bfloat16), "dp", scatter_dimension=0, tiled=True
    ).astype(jnp.float32)
    return (resid_mid.astype(jnp.float32) + ffn_out).astype(jnp.bfloat16)


def solution(mesh):
    return jax.shard_map(
        per_device,
        mesh=mesh,
        in_specs=(
            P("dp", ("section", "tensor")),
            P("dp", None),
            P(),
            P(None, ("section", "tensor")),
            P(None, ("section", "tensor")),
            P(None, ("section", "tensor")),
            P(("section", "tensor"), None),
            P(),
            P(("section", "tensor"), "dp"),
            P("dp", ("section", "tensor")),
        ),
        out_specs=P("dp", ("section", "tensor")),
        check_vma=False,
    )
```

profile of v0, /device:TPU:1, one launch (start us, length us, event | category | flops | bytes accessed | tf_op | source)
XLA Modules:
  0.0 491.9 jit_solution(8370720796275052697)
XLA Ops:
  6.5 0.7 all-gather.4.cloned.1.call-update
  7.3 0.9 fusion.18
  8.2 41.9 %all-gather.4.cloned.1.call-done = bf16[256,8192]{1,0:T(8,128)(2,1)} async-done(((bf16[256,512]{1,0:T(8,128)(2,1)}), bf16[256,8192]{1,0:T(8,128)(2,1)}) %all-gather.4.cloned.1.call-update) | async-done | bytes 4194320 | tf_op jit(solution)/shard_map/all_gather | solution.py:23
  50.1 3.5 convert_reduce_fusion
  53.7 1.8 fusion.3
  55.5 0.4 copy-done.5
  55.9 1.8 convolution_convert_fusion.4
  57.7 0.3 copy-done.2
  58.0 1.6 copy-done.6
  59.6 1.8 convolution_convert_fusion.5
  61.4 0.4 fusion.23
  61.8 0.3 fusion.8
  62.1 5.2 %convolution_convert_fusion.6 = bf16[256,256]{0,1:T(8,128)(2,1)S(1)} fusion(bf16[256,8192]{1,0:T(8,128)(2,1)} %copy-done.2, bf16[8192,256]{1,0:T(8,128)(2,1)} %param.15), kind=kOutput, calls=%fused_computation.26 | convolution fusion | flops 1073807360 | bytes 8519680 | tf_op jit(solution)/shard_map/dot_general | solution.py:28
  67.3 0.3 convolution_convert_fusion.3
  67.6 5.4 %convolution_convert_fusion = bf16[256,8192]{1,0:T(8,128)(2,1)} fusion(bf16[256,256]{0,1:T(8,128)(2,1)S(1)} %bitcast.30, bf16[256,8192]{1,0:T(8,128)(2,1)} %param.16), kind=kOutput, calls=%fused_computation.5 | convolution fusion | flops 1075838976 | bytes 8519680 | tf_op jit(solution)/shard_map/dot_general | solution.py:46
  73.0 0.2 all-gather.6.cloned.1.call-start
  73.3 0.8 dynamic-slice
  74.0 127.6 %all-reduce.2.cloned.1.call-done = bf16[256,8192]{1,0:T(8,128)(2,1)} async-done(((bf16[256,8192]{1,0:T(8,128)(2,1)}), bf16[256,8192]{1,0:T(8,128)(2,1)}) %all-reduce.2.cloned.1.call-update) | async-done | bytes 4194320 | tf_op jit(solution)/shard_map/psum | solution.py:47
  201.6 4.6 convert_reduce_fusion.1
  206.2 1.0 convert_element_type.73
  207.2 1.0 copy-done.4
  208.2 0.9 fusion.17
  209.1 0.0 reduce-scatter.3.cloned.1.call-start
  209.2 54.9 %all-gather.6.cloned.1.call-done = bf16[2048,512]{1,0:T(8,128)(2,1)} async-done(((bf16[256,512]{1,0:T(8,128)(2,1)}), bf16[2048,512]{1,0:T(8,128)(2,1)}) %all-gather.6.cloned.1.call-update) | async-done | bytes 2097168 | tf_op jit(solution)/shard_map/all_gather | solution.py:52
  264.1 8.3 %convolution_convert_fusion.1 = bf16[2048,2048]{1,0:T(8,128)(2,1)} fusion(bf16[2048,512]{1,0:T(8,128)(2,1)} %all-gather.6.cloned.1.call-done, bf16[512,2048]{1,0:T(8,128)(2,1)S(1)} %copy-done), kind=kOutput, calls=%fused_computation.12 | convolution fusion | flops 4299161600 | bytes 12582912 | tf_op jit(solution)/shard_map/dot_general | solution.py:54
  272.4 69.6 %reduce-scatter.3.cloned.1.call-done = bf16[128,2048]{1,0:T(8,128)(2,1)} async-done(((bf16[2048,2048]{1,0:T(8,128)(2,1)}), bf16[128,2048]{1,0:T(8,128)(2,1)}) %reduce-scatter.3.cloned.1.call-update) | async-done | bytes 524304 | tf_op jit(solution)/shard_map/reduce_scatter | solution.py:53
  342.1 2.2 fusion.14
  344.3 0.0 reduce-scatter.5.cloned.1.call-start
  344.4 54.7 %all-gather.8.cloned.1.call-done = bf16[2048,2048]{1,0:T(8,128)(2,1)} async-done(((bf16[128,2048]{1,0:T(8,128)(2,1)}), bf16[2048,2048]{1,0:T(8,128)(2,1)}) %all-gather.8.cloned.1.call-update) | async-done | bytes 8388624 | tf_op jit(solution)/shard_map/all_gather | solution.py:61
  399.1 10.0 %convolution_convert_fusion.2 = bf16[2048,512]{1,0:T(8,128)(2,1)} fusion(bf16[2048,2048]{1,0:T(8,128)(2,1)} %all-gather.8.cloned.1.call-done, bf16[2048,512]{1,0:T(8,128)(2,1)} %param.19), kind=kOutput, calls=%fused_computation.14 | convolution fusion | flops 4296015872 | bytes 12582912 | tf_op jit(solution)/shard_map/dot_general | solution.py:60
  409.1 74.2 %reduce-scatter.5.cloned.1.call-done = bf16[256,512]{1,0:T(8,128)(2,1)} async-done(((bf16[2048,512]{1,0:T(8,128)(2,1)}), bf16[256,512]{1,0:T(8,128)(2,1)}) %reduce-scatter.5.cloned.1.call-update) | async-done | bytes 262160 | tf_op jit(solution)/shard_map/reduce_scatter | solution.py:65
  483.3 1.8 add_convert_fusion
  (22 shorter events, 0.2 us)
Async XLA Ops:
  6.5 257.5 %copy-start = (bf16[512,2048]{1,0:T(8,128)(2,1)S(1)}, bf16[512,2048]{1,0:T(8,128)(2,1)}, u32[]{:S(2)}) copy-start(bf16[512,2048]{1,0:T(8,128)(2,1)} %param.18) | copy-start | bytes 6291460
  6.5 47.1 %copy-start.7 = (f32[8192]{0:T(1024)S(1)}, f32[8192]{0:T(1024)}, u32[]{:S(2)}) copy-start(f32[8192]{0:T(1024)} %param.12) | copy-start | bytes 98308
  6.5 43.6 %all-gather.4.cloned.1.call-start = ((), (), s32[]{:S(2)}) async-start(), calls=%async_computation.2 | async-start | bytes 4456448 | tf_op jit(solution)/shard_map/all_gather | solution.py:23
  7.3 194.4 %all-reduce.2.cloned.1.call-start = ((), (), s32[]{:S(2)}) async-start(), calls=%async_computation.3 | async-start | bytes 8388608 | tf_op jit(solution)/shard_map/psum | solution.py:47
  50.1 3.6 copy-start.3
  53.7 2.2 copy-start.5
  55.9 2.1 copy-start.2
  55.9 3.7 copy-start.6
  73.0 191.0 %all-gather.6.cloned.1.call-start = ((), (), s32[]{:S(2)}) async-start(), calls=%async_computation.4 | async-start | bytes 2359296 | tf_op jit(solution)/shard_map/all_gather | solution.py:52
  206.2 2.0 copy-start.4
  209.1 133.0 %reduce-scatter.3.cloned.1.call-start = ((), (), s32[]{:S(2)}) async-start(), calls=%async_computation.5 | async-start | bytes 8912896 | tf_op jit(solution)/shard_map/reduce_scatter | solution.py:53
  272.4 126.7 %all-gather.8.cloned.1.call-start = ((), (), s32[]{:S(2)}) async-start(), calls=%async_computation.6 | async-start | bytes 8912896 | tf_op jit(solution)/shard_map/all_gather | solution.py:61
  344.3 139.0 %reduce-scatter.5.cloned.1.call-start = ((), (), s32[]{:S(2)}) async-start(), calls=%async_computation.7 | async-start | bytes 2359296 | tf_op jit(solution)/shard_map/reduce_scatter | solution.py:65
  399.1 86.0 %copy-start.1 = (bf16[512,2048]{1,0:T(8,128)(2,1)S(1)}, bf16[512,2048]{1,0:T(8,128)(2,1)}, u32[]{:S(2)}) copy-start(bf16[512,2048]{1,0:T(8,128)(2,1)} %param.18) | copy-start | bytes 6291460
Sparse Core Ops, SparseCore 0:
  9.0 41.0 all-gather.3
  73.2 128.4 all-reduce.1
  209.2 54.7 all-gather.5
  272.5 69.5 reduce-scatter.2
  344.4 54.5 all-gather.7
  409.2 74.0 reduce-scatter.4
where the time goes:
time: 493 us; the launch traced here: 492 us
  waiting for transfers between devices  424 us (86%)
  matrix products  33.5 us (7%)
  other arithmetic  16.6 us (3%)
  between operations  13.6 us (3%)
    psum x1, waiting for transfers between devices, per_device(): lax.psum(partial_out.astype(jnp.bfloat16), ('section', 'tensor'))  128 us
    reduce_scatter x1, waiting for transfers between devices, per_device(): lax.psum_scatter(partial_down.astype(jnp.bfloat16), 'dp', scatter_dimensi...  74.2 us
    reduce_scatter x1, waiting for transfers between devices, per_device(): lax.psum_scatter(jnp.dot(gathered, w_up, preferred_element_type=jnp.float...  69.6 us
    all_gather x1, waiting for transfers between devices, per_device(): gathered = lax.all_gather(normed_ffn, 'dp', axis=0, tiled=True)  54.9 us
    all_gather x1, waiting for transfers between devices, per_device(): lax.all_gather(activated, ('section', 'tensor'), axis=0, tiled=True)  54.7 us
    all_gather x1, waiting for transfers between devices, per_device(): whole = lax.all_gather(tokens, ('section', 'tensor'), axis=1, tiled=True)  41.9 us
    dot_general x1, matrix products, per_device(): jnp.dot(lax.all_gather(activated, ('section', 'tensor'), axis=0, tiled=Tr...  9.99 us
  transfers between devices with their start and end apart: 6, of which 6 were waited for; matrix products, arithmetic and copies ran while one was open for 0% of the time, Pallas kernels for 0%

commit v1 on v0

v1 whole, which is shorter than its diff:
```python
import jax
import jax.numpy as jnp
from jax import lax
from jax.experimental import pallas as pl
from jax.experimental.pallas import tpu as pltpu
from jax.sharding import PartitionSpec as P

MESH = pl.DeviceIdType.MESH
HD = 128
F32 = jnp.float32
BF16 = jnp.bfloat16
N_G = 16
N_DP = 8


def remote(src, dst, send_sem, recv_sem, device):
    return pltpu.make_async_remote_copy(
        src_ref=src,
        dst_ref=dst,
        send_sem=send_sem,
        recv_sem=recv_sem,
        device_id=device,
        device_id_type=MESH,
    )


def rows_to_columns(row, width):
    column = jnp.transpose(jnp.broadcast_to(row, (128, row.shape[1])))
    return jnp.concatenate([column] * (width // 128), axis=1)


def partial_stats(values):
    ones = jnp.ones((8, values.shape[1]), BF16)
    dims = (((1,), (1,)), ((), ()))
    wide = values.astype(F32)
    square = wide * wide
    high = square.astype(BF16)
    low = (square - high.astype(F32)).astype(BF16)
    total = lax.dot_general(ones, values, dims, preferred_element_type=F32)
    second = lax.dot_general(ones, high, dims, preferred_element_type=F32)
    second += lax.dot_general(ones, low, dims, preferred_element_type=F32)
    return jnp.where(lax.broadcasted_iota(jnp.int32, total.shape, 0) == 0, total, second)


def attention_kernel(
    tok_ref, seg_ref, gain_a_ref, gain_f_ref, wq_hbm, wk_hbm, wv_hbm, wo_hbm,
    resid_ref, normed_ref,
    wq, wk, wv, wo, tok, acc, part, sib, land, stat_own, stats, mu, scale,
    w_sem, ag_send, ag_recv, sib_send, sib_recv, rs_send, rs_recv, st_send, st_recv,
):
    a = lax.axis_index("section")
    t = lax.axis_index("tensor")
    z, c = t // 2, t % 2
    oa, oc = 1 - a, 1 - c
    zp, zm, z2 = (z + 1) % 4, (z + 3) % 4, (z + 2) % 4
    me = a * 8 + t

    def dev(a_, z_, c_):
        return {"section": a_, "tensor": z_ * 2 + c_}

    def slot(a_, z_, c_):
        return a_ * 8 + z_ * 2 + c_

    def peer(r):
        i = (me + r) % N_G
        return i, {"section": i // 8, "tensor": i % 8}

    barrier = pltpu.get_barrier_semaphore()

    @pl.loop(1, N_G)
    def _(r):
        pl.semaphore_signal(barrier, inc=1, device_id=peer(r)[1], device_id_type=MESH)

    loads = [
        pltpu.make_async_copy(h, v, w_sem.at[n])
        for n, (h, v) in enumerate(((wq_hbm, wq), (wk_hbm, wk), (wv_hbm, wv), (wo_hbm, wo)))
    ]
    for load in loads:
        load.start()
    stat_own[0] = partial_stats(tok_ref[...])
    stats[0, me] = stat_own[0]
    tok[me] = tok_ref[...]
    pl.semaphore_wait(barrier, N_G - 1)

    def stat_copy(n, r):
        i, device = peer(r)
        return remote(stat_own.at[n], stats.at[n, me], st_send.at[n, r], st_recv.at[n, me], device)

    def stat_wait(n, r):
        i, device = peer(r)
        remote(stat_own.at[n], stats.at[n, i], st_send.at[n, r], st_recv.at[n, i], device).wait_recv()

    def exchange(n):
        @pl.loop(1, N_G)
        def _(r):
            stat_copy(n, r).start()

    def norm_of(n, width):
        @pl.loop(1, N_G)
        def _(r):
            stat_wait(n, r)

        total = jnp.sum(stats[n], axis=0)
        mean = total[0:1] / 8192.0
        second = total[1:2] / 8192.0
        inverse = lax.rsqrt(second - mean * mean + 1e-05)
        mu[...] = rows_to_columns(mean, width)
        scale[...] = rows_to_columns(inverse, width)

    def ag(n, s, device):
        return remote(tok.at[s], tok.at[s], ag_send.at[n], ag_recv.at[s], device)

    own = slot(a, z, c)
    exchange(0)
    sends = []

    def go(copy):
        copy.start()
        sends.append(copy)

    def arrived(s):
        ag(0, s, dev(a, zp, c)).wait_recv()

    def to_sib(n, s):
        go(ag(n, s, dev(a, z, oc)))

    go(ag(0, own, dev(oa, z, c)))
    go(ag(1, own, dev(a, zp, c)))
    go(ag(2, own, dev(a, zm, c)))
    to_sib(3, own)
    go(ag(4, own, dev(a, z2, c)))
    norm_of(0, 512)
    acc[...] = jnp.zeros_like(acc)

    def project(s):
        x = (tok[s].astype(F32) - mu[...]) * scale[...] * gain_a_ref[s]
        x = x.astype(BF16)
        at = pl.ds(pl.multiple_of(s * 512, 512), 512)
        for n, w in enumerate((wq, wk, wv)):
            acc[:, n * 256 : (n + 1) * 256] += jnp.dot(x, w[at, :], preferred_element_type=F32)

    for load in loads[:3]:
        load.wait()
    project(own)
    s_x, s_zp, s_zm, s_z2 = slot(oa, z, c), slot(a, zp, c), slot(a, zm, c), slot(a, z2, c)
    s_xzp, s_xzm, s_xz2 = slot(oa, zp, c), slot(oa, zm, c), slot(oa, z2, c)
    arrived(slot(a, z, oc))
    project(slot(a, z, oc))
    arrived(s_x)
    go(ag(5, s_x, dev(a, zp, c)))
    go(ag(6, s_x, dev(a, zm, c)))
    to_sib(7, s_x)
    project(s_x)
    arrived(s_zp)
    to_sib(8, s_zp)
    project(s_zp)
    arrived(s_zm)
    to_sib(9, s_zm)
    project(s_zm)
    arrived(slot(oa, z, oc))
    project(slot(oa, z, oc))
    arrived(slot(a, zp, oc))
    project(slot(a, zp, oc))
    arrived(slot(a, zm, oc))
    project(slot(a, zm, oc))
    arrived(s_z2)
    go(ag(10, s_z2, dev(oa, z, c)))
    to_sib(11, s_z2)
    project(s_z2)
    arrived(slot(a, z2, oc))
    project(slot(a, z2, oc))
    for n, s in ((12, s_xzp), (13, s_xzm), (14, s_xz2)):
        arrived(s)
        to_sib(n, s)
        project(s)
    for z_ in (zp, zm, z2):
        arrived(slot(oa, z_, oc))
        project(slot(oa, z_, oc))

    rows = tok_ref.shape[0]
    seg_row = seg_ref[...].astype(F32)
    seg_col = rows_to_columns(seg_row, rows)
    at_q = lax.broadcasted_iota(jnp.int32, (rows, rows), 0)
    at_k = lax.broadcasted_iota(jnp.int32, (rows, rows), 1)
    keep = jnp.logical_and(at_q >= at_k, seg_col == seg_row)
    contexts = []
    for head in range(2):
        q, k, v = (
            acc[:, n * 256 + head * HD : n * 256 + (head + 1) * HD].astype(BF16) for n in range(3)
        )
        scores = lax.dot_general(q, k, (((1,), (1,)), ((), ())), preferred_element_type=F32)
        scores = jnp.where(keep, scores * HD ** (-0.5), -1e30)
        expo = jnp.exp(scores - jnp.max(scores, axis=-1, keepdims=True))
        probs = (expo / jnp.sum(expo, axis=-1, keepdims=True)).astype(BF16)
        contexts.append(jnp.dot(probs, v, preferred_element_type=F32).astype(BF16))
    context = jnp.concatenate(contexts, axis=1)
    loads[3].wait()

    def term(s):
        at = pl.ds(pl.multiple_of(s * 512, 512), 512)
        return jnp.dot(context, wo[:, at], preferred_element_type=F32)

    order = ((oa, z2), (oa, zp), (oa, zm), (a, zp), (a, zm), (a, z2), (oa, z), (a, z))

    def sib_copy(n):
        a_, z_ = order[n]
        return remote(part.at[oc, n], sib.at[n], sib_send.at[n], sib_recv.at[n], dev(a, z, oc))

    def pair(n):
        a_, z_ = order[n]
        mine = term(slot(a_, z_, c))
        sib_copy(n).wait_recv()
        return mine + sib[n].astype(F32)

    for n, (a_, z_) in enumerate(order):
        part[oc, n] = term(slot(a_, z_, oc)).astype(BF16)
        go(sib_copy(n))

    def reduce_copy(n, device):
        return remote(part.at[c, n], land.at[n], rs_send.at[n], rs_recv.at[n], device)

    targets = (
        dev(oa, z, c), dev(a, zp, c), dev(a, zm, c), dev(a, zp, c), dev(a, zm, c),
        dev(a, z2, c), dev(oa, z, c),
    )
    for n in range(5):
        part[c, n] = pair(n).astype(BF16)
        go(reduce_copy(n, targets[n]))
    far, across, mine = pair(5), pair(6), pair(7)

    def landed(n):
        reduce_copy(n, targets[n]).wait_recv()
        return land[n].astype(F32)

    part[c, 5] = (far + landed(0)).astype(BF16)
    go(reduce_copy(5, targets[5]))
    part[c, 6] = (across + landed(1) + landed(2)).astype(BF16)
    go(reduce_copy(6, targets[6]))
    total = mine + landed(3) + landed(4) + landed(6) + landed(5)
    resid = (tok_ref[...].astype(F32) + total).astype(BF16)
    resid_ref[...] = resid
    stat_own[1] = partial_stats(resid)
    stats[1, me] = stat_own[1]
    exchange(1)
    norm_of(1, 512)
    normed = (resid.astype(F32) - mu[...]) * scale[...] * gain_f_ref[me]
    normed_ref[...] = normed.astype(BF16)

    for copy in sends:
        copy.wait_send()
    for n in range(2):

        @pl.loop(1, N_G)
        def _(r):
            stat_copy(n, r).wait_send()


def attention(tokens, segment_ids, gain_attn, gain_ffn, w_query, w_key, w_value, w_output):
    rows, share = tokens.shape
    vmem, hbm = pl.BlockSpec(memory_space=pltpu.VMEM), pl.BlockSpec(memory_space=pl.ANY)
    out = jax.ShapeDtypeStruct((rows, share), BF16)
    return pl.pallas_call(
        attention_kernel,
        out_shape=(out, out),
        in_specs=[vmem] * 4 + [hbm] * 4,
        out_specs=(vmem, vmem),
        scratch_shapes=[
            pltpu.VMEM(w_query.shape, BF16),
            pltpu.VMEM(w_query.shape, BF16),
            pltpu.VMEM(w_query.shape, BF16),
            pltpu.VMEM(w_output.shape, BF16),
            pltpu.VMEM((N_G, rows, share), BF16),
            pltpu.VMEM((rows, 768), F32),
            pltpu.VMEM((2, 8, rows, share), BF16),
            pltpu.VMEM((8, rows, share), BF16),
            pltpu.VMEM((7, rows, share), BF16),
            pltpu.VMEM((2, 8, rows), F32),
            pltpu.VMEM((2, N_G, 8, rows), F32),
            pltpu.VMEM((rows, share), F32),
            pltpu.VMEM((rows, share), F32),
            pltpu.SemaphoreType.DMA((4,)),
            pltpu.SemaphoreType.DMA((15,)),
            pltpu.SemaphoreType.DMA((N_G,)),
            pltpu.SemaphoreType.DMA((8,)),
            pltpu.SemaphoreType.DMA((8,)),
            pltpu.SemaphoreType.DMA((7,)),
            pltpu.SemaphoreType.DMA((7,)),
            pltpu.SemaphoreType.DMA((2, N_G)),
            pltpu.SemaphoreType.DMA((2, N_G)),
        ],
        compiler_params=pltpu.CompilerParams(
            collective_id=0, has_side_effects=True, vmem_limit_bytes=48 << 20
        ),
        name="attention",
    )(
        tokens, segment_ids, gain_attn.reshape(N_G, 1, share), gain_ffn.reshape(N_G, 1, share),
        w_query, w_key, w_value, w_output,
    )


SB, RX1, RZP, RZM, FZP, FZM, FZ2, FX, AZP, AZM, AZ2, AX, XZP, XZM, XZ2, AS = range(16)


def ffn_kernel(
    n_ref, r_ref, wu_hbm, wd_hbm,
    o_ref,
    wu, wd, nb, up, sb, land, act, down, fin,
    w_sem, send, recv, nb_send, nb_recv, dp_send, dp_recv,
):
    a = lax.axis_index("section")
    t = lax.axis_index("tensor")
    d = lax.axis_index("dp")
    z, c = t // 2, t % 2
    xh, y = d // 4, d % 4
    oa, oc = 1 - a, 1 - c
    zp, zm, z2 = (z + 1) % 4, (z + 3) % 4, (z + 2) % 4

    def dev(a_, z_, c_):
        return {"section": a_, "tensor": z_ * 2 + c_}

    D_X, D_ZP, D_ZM, D_Z2, D_S = dev(oa, z, c), dev(a, zp, c), dev(a, zm, c), dev(a, z2, c), dev(a, z, oc)

    def at_dp(d_):
        return {"dp": d_}

    def dp_of(k):
        dx = ((k + 1) // 4) % 2
        dy = ((k + 1) % 4 + 3 - 3 * dx) % 4
        return ((xh + dx) % 2) * 4 + (y + dy) % 4

    barrier = pltpu.get_barrier_semaphore()
    for device in (D_X, D_ZP, D_ZM, D_Z2, D_S):
        pl.semaphore_signal(barrier, inc=1, device_id=device, device_id_type=MESH)

    @pl.loop(1, N_DP)
    def _(r):
        pl.semaphore_signal(barrier, inc=1, device_id=at_dp((d + r) % N_DP), device_id_type=MESH)

    loads = [
        pltpu.make_async_copy(wu_hbm, wu, w_sem.at[0]),
        pltpu.make_async_copy(wd_hbm, wd, w_sem.at[1]),
    ]
    for load in loads:
        load.start()
    nb[d] = n_ref[...]
    pl.semaphore_wait(barrier, 5 + N_DP - 1)

    def nb_copy(n, s, device):
        return remote(nb.at[s], nb.at[s], nb_send.at[n], nb_recv.at[s], device)

    def y_of(dy):
        return xh * 4 + (y + dy) % 4

    across = (1 - xh) * 4 + y
    nb_sends = [
        nb_copy(0, d, at_dp(y_of(1))),
        nb_copy(1, d, at_dp(y_of(3))),
        nb_copy(2, d, at_dp(across)),
        nb_copy(3, d, at_dp(y_of(2))),
    ]
    nb_forwards = [nb_copy(3 + dy, across, at_dp(y_of(dy))) for dy in (1, 2, 3)]
    for copy in nb_sends:
        copy.start()

    def block(k, a_, z_):
        return up.at[k, c, a_ * 4 + z_]

    def act_block(k, a_, z_):
        return act.at[k, c, a_ * 4 + z_]

    def copy_of(kind, k):
        b = land.at[k, kind - 1] if RX1 <= kind <= FX else None
        src, dst, device = {
            SB: lambda: (up.at[k, oc], sb.at[k], D_S),
            RX1: lambda: (block(k, oa, z2), b, D_X),
            RZP: lambda: (block(k, oa, zp), b, D_ZP),
            RZM: lambda: (block(k, oa, zm), b, D_ZM),
            FZP: lambda: (block(k, a, zp), b, D_ZP),
            FZM: lambda: (block(k, a, zm), b, D_ZM),
            FZ2: lambda: (block(k, a, z2), b, D_Z2),
            FX: lambda: (block(k, oa, z), b, D_X),
            AZP: lambda: (act_block(k, a, z),) * 2 + (D_ZP,),
            AZM: lambda: (act_block(k, a, z),) * 2 + (D_ZM,),
            AZ2: lambda: (act_block(k, a, z),) * 2 + (D_Z2,),
            AX: lambda: (act_block(k, a, z),) * 2 + (D_X,),
            XZP: lambda: (act_block(k, oa, z),) * 2 + (D_ZP,),
            XZM: lambda: (act_block(k, oa, z),) * 2 + (D_ZM,),
            XZ2: lambda: (act_block(k, a, z2),) * 2 + (D_X,),
            AS: lambda: (act.at[k, c], act.at[k, c], D_S),
        }[kind]()
        return remote(src, dst, send.at[k, kind], recv.at[k, kind], device)

    def arrived(kind, k):
        if kind < AZP:
            copy_of(kind, k).wait_recv()
            return
        ref = {
            AZP: lambda: act_block(k, a, zm),
            AZM: lambda: act_block(k, a, zp),
            AZ2: lambda: act_block(k, a, z2),
            AX: lambda: act_block(k, oa, z),
            XZP: lambda: act_block(k, oa, zm),
            XZM: lambda: act_block(k, oa, zp),
            XZ2: lambda: act_block(k, oa, z2),
            AS: lambda: act.at[k, oc],
        }[kind]()
        remote(ref, ref, send.at[k, kind], recv.at[k, kind], D_X).wait_recv()

    def landed(kind, k):
        arrived(kind, k)
        return land[k, kind - 1].astype(F32)

    def up_product(k):
        s = dp_of(k)

        @pl.when(jnp.logical_and(k != 0, k != 3))
        def _():
            nb_copy(0, s, at_dp(across)).wait_recv()

        @pl.when(k == 2)
        def _():
            nb_copy(0, across, at_dp(across)).wait_recv()
            for copy in nb_forwards:
                copy.start()

        x = nb[s]
        for n in range(4):
            cols = slice(n * 512, (n + 1) * 512)
            r = jnp.dot(x, wu[:, cols], preferred_element_type=F32)
            up[k, :, :, :, cols] = r.astype(BF16).reshape(2, 8, 16, 512)
        copy_of(SB, k).start()

    def pair_sum(k):
        arrived(SB, k)
        up[k, c] = (up[k, c].astype(F32) + sb[k].astype(F32)).astype(BF16)
        for kind in (RX1, RZP, RZM, FZP, FZM):
            copy_of(kind, k).start()

    def second_sum(k):
        b = a * 4 + z2
        up[k, c, b] = (up[k, c, b].astype(F32) + landed(RX1, k)).astype(BF16)
        copy_of(FZ2, k).start()
        b = oa * 4 + z
        up[k, c, b] = (up[k, c, b].astype(F32) + landed(RZP, k) + landed(RZM, k)).astype(BF16)
        copy_of(FX, k).start()

    def activate(k):
        b = a * 4 + z
        pre = up[k, c, b].astype(F32) + landed(FZP, k) + landed(FZM, k) + landed(FZ2, k) + landed(FX, k)
        inner = 0.7978845608028654 * (pre + 0.044715 * (pre * pre * pre))
        act[k, c, b] = (0.5 * pre * (1.0 + jnp.tanh(inner))).astype(BF16)
        for kind in (AX, AZP, AZM, AZ2):
            copy_of(kind, k).start()

    def spread(k):
        arrived(AX, k)
        copy_of(XZP, k).start()
        copy_of(XZM, k).start()
        arrived(AZ2, k)
        copy_of(XZ2, k).start()

    def to_sibling(k):
        for kind in (AZP, AZM, XZP, XZM, XZ2):
            arrived(kind, k)
        copy_of(AS, k).start()

    def dp_copy(k):
        return remote(down.at[k], fin.at[d], dp_send.at[k], dp_recv.at[d], at_dp(dp_of(k)))

    def down_product(k):
        arrived(AS, k)
        x = act[k].reshape(256, 2048)
        down[k] = jnp.dot(x, wd[...], preferred_element_type=F32).astype(BF16)

        @pl.when(k > 0)
        def _():
            dp_copy(k).start()

    loads[0].wait()
    up_product(0)
    loads[1].wait()

    @pl.loop(0, N_DP + 4)
    def _(step):
        def stage(f, lag):
            k = step - lag

            @pl.when(jnp.logical_and(k >= 0, k < N_DP))
            def _():
                f(k)

        stage(pair_sum, 0)
        stage(second_sum, 1)
        stage(activate, 2)
        stage(spread, 3)
        stage(to_sibling, 4)
        stage(up_product, -1)
        stage(down_product, 4)

    total = r_ref[...].astype(F32) + down[0].astype(F32)
    for r in range(1, N_DP):
        s = (d + r) % N_DP
        remote(down.at[0], fin.at[s], dp_send.at[0], dp_recv.at[s], at_dp(across)).wait_recv()
        total += fin[s].astype(F32)
    o_ref[...] = total.astype(BF16)

    for copy in nb_sends + nb_forwards:
        copy.wait_send()

    @pl.loop(0, N_DP)
    def _(k):
        for kind in range(16):
            copy_of(kind, k).wait_send()

        @pl.when(k > 0)
        def _():
            dp_copy(k).wait_send()


def ffn(normed, resid, w_up, w_down):
    rows, share = normed.shape
    vmem, hbm = pl.BlockSpec(memory_space=pltpu.VMEM), pl.BlockSpec(memory_space=pl.ANY)
    hid = w_up.shape[1]
    return pl.pallas_call(
        ffn_kernel,
        out_shape=jax.ShapeDtypeStruct((rows, share), BF16),
        in_specs=[vmem, vmem, hbm, hbm],
        out_specs=vmem,
        scratch_shapes=[
            pltpu.VMEM(w_up.shape, BF16),
            pltpu.VMEM(w_down.shape, BF16),
            pltpu.VMEM((N_DP, rows, share), BF16),
            pltpu.VMEM((N_DP, 2, 8, 16, hid), BF16),
            pltpu.VMEM((N_DP, 8, 16, hid), BF16),
            pltpu.VMEM((N_DP, 7, 16, hid), BF16),
            pltpu.VMEM((N_DP, 2, 8, 16, hid), BF16),
            pltpu.VMEM((N_DP, rows, share), BF16),
            pltpu.VMEM((N_DP, rows, share), BF16),
            pltpu.SemaphoreType.DMA((2,)),
            pltpu.SemaphoreType.DMA((N_DP, 16)),
            pltpu.SemaphoreType.DMA((N_DP, 16)),
            pltpu.SemaphoreType.DMA((7,)),
            pltpu.SemaphoreType.DMA((N_DP,)),
            pltpu.SemaphoreType.DMA((N_DP,)),
            pltpu.SemaphoreType.DMA((N_DP,)),
        ],
        compiler_params=pltpu.CompilerParams(
            collective_id=1, has_side_effects=True, vmem_limit_bytes=52 << 20
        ),
        name="ffn",
    )(normed, resid, w_up, w_down)


def per_device(
    tokens, segment_ids, gain_attn, w_query, w_key, w_value, w_output, gain_ffn, w_up, w_down
):
    resid, normed = attention(
        tokens, segment_ids, gain_attn, gain_ffn, w_query, w_key, w_value, w_output
    )
    return ffn(normed, resid, w_up, w_down)


def solution(mesh):
    return jax.shard_map(
        per_device,
        mesh=mesh,
        in_specs=(
            P("dp", ("section", "tensor")),
            P("dp", None),
            P(),
            P(None, ("section", "tensor")),
            P(None, ("section", "tensor")),
            P(None, ("section", "tensor")),
            P(("section", "tensor"), None),
            P(),
            P(("section", "tensor"), "dp"),
            P("dp", ("section", "tensor")),
        ),
        out_specs=P("dp", ("section", "tensor")),
        check_vma=False,
    )
```

time: 493 us -> 175 us (0.35)
  waiting for transfers between devices: 424 us -> 0 us
  Pallas kernels: 0 us -> 169 us
  matrix products: 33.5 us -> 0 us
  other arithmetic: 16.6 us -> 0 us
  between operations: 13.6 us -> 0.02 us
    pallas_call x0 -> x2, Pallas kernels: none -> 169 us  [the longest x1 109 us: ffn(): pl.pallas_call(ffn_kernel, out_shape=jax.ShapeDtypeStruct((rows, share),...]
    all_gather x3 -> x0, waiting for transfers between devices: 152 us -> none  [the longest x1 54.9 us: per_device(): gathered = lax.all_gather(normed_ffn, 'dp', axis=0, tiled=True)]
    reduce_scatter x2 -> x0, waiting for transfers between devices: 144 us -> none  [the longest x1 74.2 us: per_device(): lax.psum_scatter(partial_down.astype(jnp.bfloat16), 'dp', scatter_dimensi...]
    psum x1 -> x0, waiting for transfers between devices: 128 us -> none  [per_device(): lax.psum(partial_out.astype(jnp.bfloat16), ('section', 'tensor'))]
    dot_general x8 -> x0, matrix products: 33.2 us -> none  [the longest x1 9.99 us: per_device(): jnp.dot(lax.all_gather(activated, ('section', 'tensor'), axis=0, tiled=Tr...]
    reduce_sum x2 -> x0, other arithmetic: 8.11 us -> none  [layer_norm(): mean = jnp.mean(values, axis=-1, keepdims=True)]
    convert_element_type x5 -> x0, other arithmetic: 7.66 us -> none  [the longest x1 2.23 us: per_device(): activated = jax.nn.gelu(pre_act, approximate=True).astype(jnp.bfloat16)]
  transfers between devices with their start and end apart: 6 -> 0, of which waited for: 6 -> 0; matrix products, arithmetic and copies ran while one was open for 0% -> 0% of each run, Pallas kernels for 0% -> 0%
where the time goes in v1:
time: 175 us
  Pallas kernels  169 us (97%)
  local copies, waits for them, and re-layouts  6.04 us (3%)
    pallas_call x1, Pallas kernels, ffn(): pl.pallas_call(ffn_kernel, out_shape=jax.ShapeDtypeStruct((rows, share),...  109 us
    pallas_call x1, Pallas kernels, attention(): pl.pallas_call(attention_kernel, out_shape=(out, out), in_specs=[vmem] *...  59.8 us
    unnamed x11, local copies, waits for them, and re-layouts  6.04 us

profile of v1, /device:TPU:1, one launch (start us, length us, event | category | flops | bytes accessed | tf_op | source)
XLA Modules:
  0.0 174.9 jit_solution(4342406745270725570)
XLA Ops:
  0.0 0.0 copy-start
  0.0 2.2 %copy-done = bf16[8192,256]{1,0:T(8,128)(2,1)S(1)} copy-done((bf16[8192,256]{1,0:T(8,128)(2,1)S(1)}, bf16[8192,256]{1,0:T(8,128)(2,1)}, u32[]{:S(2)}) %copy-start) | copy-done | bytes 4194328
  2.2 0.0 copy-start.1
  2.2 0.9 copy-done.1
  3.1 0.0 copy-start.2
  3.1 0.8 copy-done.2
  3.9 0.0 copy-start.3
  3.9 0.8 copy-done.3
  4.7 0.0 copy-start.4
  4.7 0.7 copy-done.4
  5.3 59.8 %attention.1 = (bf16[256,512]{1,0:T(8,128)(2,1)S(1)}, bf16[256,512]{1,0:T(8,128)(2,1)S(1)}) custom-call(bf16[256,512]{1,0:T(8,128)(2,1)S(1)} %copy-done.1, s32[1,256]{1,0:T(1,128)S(1)} %copy-done.4, f32[16,1,512]{2,1,0:T(1,128)S(1)} %bitcast.2, f32[16,1,512]{2,1,0:T(1,128)S(1)} %bitcast.3, bf16[8192,256]{1,0:T(8,128)(2,1)S(1)} %copy-done, ...), custom_call_target="tpu_custom_call" | custom-call | tf_op jit(solution)/shard_map/attention/pallas_call | solution.py:262
  65.2 109.0 %ffn.1 = bf16[256,512]{1,0:T(8,128)(2,1)S(1)} custom-call(bf16[256,512]{1,0:T(8,128)(2,1)S(1)} %get-tuple-element.7.n_ref, bf16[256,512]{1,0:T(8,128)(2,1)S(1)} %get-tuple-element.8.r_ref, bf16[512,2048]{1,0:T(8,128)(2,1)} %wu_hbm.1, bf16[2048,512]{1,0:T(8,128)(2,1)} %wd_hbm.1), custom_call_target="tpu_custom_call" | custom-call | tf_op jit(solution)/shard_map/ffn/pallas_call | solution.py:524
  174.2 0.7 copy.12
Async XLA Ops:
  0.0 2.2 %copy-start = (bf16[8192,256]{1,0:T(8,128)(2,1)S(1)}, bf16[8192,256]{1,0:T(8,128)(2,1)}, u32[]{:S(2)}) copy-start(bf16[8192,256]{1,0:T(8,128)(2,1)} %wq_hbm.1) | copy-start | bytes 12582916
  2.2 0.9 copy-start.1
  3.1 0.8 copy-start.2
  3.9 0.8 copy-start.3
  4.7 0.7 copy-start.4

commit v2 on v0

v2 whole, which is shorter than its diff:
```python
import jax
import jax.numpy as jnp
from jax import lax
from jax.experimental import pallas as pl
from jax.experimental.pallas import tpu as pltpu
from jax.sharding import PartitionSpec as P

MESH = pl.DeviceIdType.MESH
HD = 128
F32 = jnp.float32
BF16 = jnp.bfloat16
N_G = 16
N_DP = 8
HALF = 128
WIDE = 512

CHUNKS = (
    (0, 0), (0, 3), (0, 1), (0, 2), (0, 7), (0, 6), (1, 3), (1, 1),
    (0, 5), (1, 7), (1, 6), (1, 5), (0, 4), (1, 2), (1, 4), (1, 0),
)
N_K = len(CHUNKS)
CHUNK_OF = {chunk: k for k, chunk in enumerate(CHUNKS)}
FORWARD_AT = (2, 7)
DIRECT_SUM = 6
DIRECT_GATHER = 11
RING = 8

(
    SB, RX1, RZP, RZM, FX, FZP1, FZM0, H0, H1, FZP0, FZM1, FZP, FZM, FZ2,
    AX, AZP, AZM, XZP, XZM, XZ2, AS, ZH0, ZH1, AZ2,
) = range(24)
KINDS = 24
L_RX1, L_RZP, L_RZM, L_FX, L_FZP, L_FZM, L_H = range(7)


def remote(src, dst, send_sem, recv_sem, device):
    return pltpu.make_async_remote_copy(
        src_ref=src,
        dst_ref=dst,
        send_sem=send_sem,
        recv_sem=recv_sem,
        device_id=device,
        device_id_type=MESH,
    )


def pick(k, values):
    result = jnp.int32(values[0])
    for i, value in enumerate(values[1:], 1):
        result = jnp.where(k == i, jnp.int32(value), result)
    return result


def rows_to_columns(row, width):
    column = jnp.transpose(jnp.broadcast_to(row, (128, row.shape[1])))
    return jnp.concatenate([column] * (width // 128), axis=1)


def partial_stats(values):
    ones = jnp.ones((8, values.shape[1]), BF16)
    dims = (((1,), (1,)), ((), ()))
    wide = values.astype(F32)
    square = wide * wide
    high = square.astype(BF16)
    low = (square - high.astype(F32)).astype(BF16)
    total = lax.dot_general(ones, values, dims, preferred_element_type=F32)
    second = lax.dot_general(ones, high, dims, preferred_element_type=F32)
    second += lax.dot_general(ones, low, dims, preferred_element_type=F32)
    return jnp.where(lax.broadcasted_iota(jnp.int32, total.shape, 0) == 0, total, second)


def kernel(
    tok_hbm, seg_hbm, gain_a_hbm, gain_f_hbm, wq_hbm, wk_hbm, wv_hbm, wo_hbm, wu_hbm, wd_hbm,
    o_ref,
    seg, gain_a, gain_f, wq, wk, wv, wo, wu, wd,
    tok, acc, ctx, part, sib, red, own_a, own_f, stats_a, stats_f, mu, scale, resid,
    nb, up, sb, land, act, part_down, down, fin,
    w_sem, ag_send, ag_recv, sib_send, sib_recv, red_send, red_recv, sa_send, sa_recv, sf_send, sf_recv,
    send, recv, nb_send, nb_recv, dp_send, dp_recv,
):
    a = lax.axis_index("section")
    t = lax.axis_index("tensor")
    d = lax.axis_index("dp")
    z, c = t // 2, t % 2
    xh, y = d // 4, d % 4
    oa, oc = 1 - a, 1 - c
    zp, zm, z2 = (z + 1) % 4, (z + 3) % 4, (z + 2) % 4
    me = a * 8 + t

    def dev(a_, z_, c_):
        return {"section": a_, "tensor": z_ * 2 + c_}

    def slot(a_, z_, c_):
        return a_ * 8 + z_ * 2 + c_

    def at_dp(d_):
        return {"dp": d_}

    def y_of(dy):
        return xh * 4 + (y + dy) % 4

    def peer(r):
        i = (me + r) % N_G
        return i, {"section": i // 8, "tensor": i % 8}

    D_X, D_ZP, D_ZM = dev(oa, z, c), dev(a, zp, c), dev(a, zm, c)
    D_Z2, D_S = dev(a, z2, c), dev(a, z, oc)
    across = (1 - xh) * 4 + y
    dp_peers = [at_dp(y_of(dy)) for dy in (1, 2, 3)] + [at_dp(across)]

    barrier = pltpu.get_barrier_semaphore()

    @pl.loop(1, N_G)
    def _(r):
        pl.semaphore_signal(barrier, inc=1, device_id=peer(r)[1], device_id_type=MESH)

    for device in dp_peers:
        pl.semaphore_signal(barrier, inc=1, device_id=device, device_id_type=MESH)

    pairs = (
        (tok_hbm, tok.at[me]), (gain_a_hbm, gain_a), (seg_hbm, seg), (gain_f_hbm.at[me], gain_f),
        (wq_hbm, wq), (wk_hbm, wk), (wv_hbm, wv), (wo_hbm, wo), (wu_hbm, wu), (wd_hbm, wd),
    )
    loads = [pltpu.make_async_copy(h, v, w_sem.at[n]) for n, (h, v) in enumerate(pairs)]
    for load in loads:
        load.start()
    loads[0].wait()
    for h in range(2):
        own_a[h] = partial_stats(tok[me, h])
    stats_a[me] = own_a[...]
    pl.semaphore_wait(barrier, N_G - 1 + len(dp_peers))

    sends = []

    def go(copy):
        copy.start()
        sends.append(copy)

    def stat_a(r):
        i, device = peer(r)
        return remote(own_a, stats_a.at[me], sa_send.at[r], sa_recv.at[me], device)

    def stat_f(h, r):
        i, device = peer(r)
        return remote(own_f.at[h], stats_f.at[h, me], sf_send.at[h, r], sf_recv.at[h, me], device)

    @pl.loop(1, N_G)
    def _(r):
        stat_a(r).start()

    def norm_from(total, h):
        mean = total[0:1] / 8192.0
        second = total[1:2] / 8192.0
        inverse = lax.rsqrt(second - mean * mean + 1e-05)
        mu[h] = rows_to_columns(mean, WIDE)
        scale[h] = rows_to_columns(inverse, WIDE)

    ags = []

    def ag(s, h, device):
        n = len(ags)
        ags.append(remote(tok.at[s, h], tok.at[s, h], ag_send.at[n], ag_recv.at[s, h], device))
        go(ags[n])

    def arrived(s, h):
        remote(tok.at[s, h], tok.at[s, h], ag_send.at[0], ag_recv.at[s, h], D_X).wait_recv()

    s_own, s_x, s_zp, s_zm = slot(a, z, c), slot(oa, z, c), slot(a, zp, c), slot(a, zm, c)
    s_z2, s_xzp, s_xzm, s_xz2 = slot(a, z2, c), slot(oa, zp, c), slot(oa, zm, c), slot(oa, z2, c)

    def other(s):
        return s + oc - c

    def project(s, h):
        x = (tok[s, h].astype(F32) - mu[h]) * scale[h] * gain_a[s]
        x = x.astype(BF16)
        at = pl.ds(pl.multiple_of(s * WIDE, WIDE), WIDE)
        for n, w in enumerate((wq, wk, wv)):
            acc[h, :, n * 256 : (n + 1) * 256] += jnp.dot(x, w[at, :], preferred_element_type=F32)

    def t_x(h):
        ag(s_own, h, D_X)

    def t_zz(h):
        ag(s_own, h, D_ZP)
        ag(s_own, h, D_ZM)

    def t_s(h):
        ag(s_own, h, D_S)

    def t_z2(h):
        ag(s_own, h, D_Z2)

    def t_fx(h):
        arrived(s_x, h)
        ag(s_x, h, D_ZP)
        ag(s_x, h, D_ZM)
        ag(s_x, h, D_S)

    def t_fz(h):
        for s in (s_zp, s_zm):
            arrived(s, h)
            ag(s, h, D_S)

    def t_f2(h):
        arrived(s_z2, h)
        ag(s_z2, h, D_X)
        ag(s_z2, h, D_S)

    def t_f3(h):
        for s in (s_xzp, s_xzm):
            arrived(s, h)
            ag(s, h, D_S)

    def t_f4(h):
        arrived(s_xz2, h)
        ag(s_xz2, h, D_S)

    def t_norm(h):
        if h == 0:

            @pl.loop(1, N_G)
            def _(r):
                i, device = peer(r)
                remote(own_a, stats_a.at[i], sa_send.at[r], sa_recv.at[i], device).wait_recv()

            for n in range(2):
                norm_from(jnp.sum(stats_a[:, n], axis=0), n)
            acc[...] = jnp.zeros_like(acc)
            for n in (1, 2, 3, 4, 5, 6):
                loads[n].wait()

    def t_p0(h):
        project(s_own, h)
        arrived(other(s_own), h)
        project(other(s_own), h)

    def t_px(h):
        project(s_x, h)

    def t_pz(h):
        project(s_zp, h)
        project(s_zm, h)

    def t_p2(h):
        project(s_z2, h)

    def t_p3(h):
        project(s_xzp, h)
        project(s_xzm, h)

    def t_p4(h):
        project(s_xz2, h)

    def others(h, *slots):
        for s in slots:
            arrived(other(s), h)
            project(other(s), h)

    def t_qx(h):
        others(h, s_x)

    def t_qz(h):
        others(h, s_zp, s_zm)

    def t_q2(h):
        others(h, s_z2)

    def t_q3(h):
        others(h, s_xzp, s_xzm)

    def t_q4(h):
        others(h, s_xz2)

    def t_att(h):
        keys = (h + 1) * HALF
        seg_row = seg[...].astype(F32)
        seg_col = rows_to_columns(seg_row[:, h * HALF : (h + 1) * HALF], keys)
        at_q = lax.broadcasted_iota(jnp.int32, (HALF, keys), 0) + h * HALF
        at_k = lax.broadcasted_iota(jnp.int32, (HALF, keys), 1)
        keep = jnp.logical_and(at_q >= at_k, seg_col == seg_row[:, :keys])
        for head in range(2):

            def part_of(n, halves):
                cols = slice(n * 256 + head * HD, n * 256 + (head + 1) * HD)
                return jnp.concatenate([acc[i, :, cols].astype(BF16) for i in halves], axis=0)

            q, k, v = part_of(0, (h,)), part_of(1, range(h + 1)), part_of(2, range(h + 1))
            scores = lax.dot_general(q, k, (((1,), (1,)), ((), ())), preferred_element_type=F32)
            scores = jnp.where(keep, scores * HD ** (-0.5), -1e30)
            expo = jnp.exp(scores - jnp.max(scores, axis=-1, keepdims=True))
            probs = (expo / jnp.sum(expo, axis=-1, keepdims=True)).astype(BF16)
            context = jnp.dot(probs, v, preferred_element_type=F32)
            ctx[h, :, head * HD : (head + 1) * HD] = context.astype(BF16)

    order = ((oa, z2), (oa, zp), (oa, zm), (a, zp), (a, zm), (a, z2), (oa, z), (a, z))

    def term(s, h):
        at = pl.ds(pl.multiple_of(s * WIDE, WIDE), WIDE)
        return jnp.dot(ctx[h], wo[:, at], preferred_element_type=F32)

    def sib_copy(n, h):
        return remote(part.at[oc, n, h], sib.at[n, h], sib_send.at[n, h], sib_recv.at[n, h], D_S)

    def t_opa(h):
        if h == 0:
            loads[7].wait()
        for n, (a_, z_) in enumerate(order):
            part[oc, n, h] = term(slot(a_, z_, oc), h).astype(BF16)
            go(sib_copy(n, h))

    red_to = (D_X, D_ZP, D_ZM, D_ZP, D_ZM, D_Z2, D_X)

    def red_copy(n, h):
        return remote(part.at[c, n, h], red.at[n, h], red_send.at[n, h], red_recv.at[n, h], red_to[n])

    def t_opb(h):
        for n, (a_, z_) in enumerate(order):
            mine = term(slot(a_, z_, c), h)
            sib_copy(n, h).wait_recv()
            part[c, n, h] = (mine + sib[n, h].astype(F32)).astype(BF16)
            if n < 5:
                go(red_copy(n, h))

    def add_landed(n, h, *landings):
        total = part[c, n, h].astype(F32)
        for i in landings:
            red_copy(i, h).wait_recv()
            total += red[i, h].astype(F32)
        return total

    def t_r1(h):
        part[c, 5, h] = add_landed(5, h, 0).astype(BF16)
        go(red_copy(5, h))

    def t_r1b(h):
        part[c, 6, h] = add_landed(6, h, 1, 2).astype(BF16)
        go(red_copy(6, h))

    def t_r3(h):
        total = tok[me, h].astype(F32) + add_landed(7, h, 3, 4, 6, 5)
        resid[h] = total.astype(BF16)
        own_f[h] = partial_stats(resid[h])
        stats_f[h, me] = own_f[h]

        @pl.loop(1, N_G)
        def _(r):
            stat_f(h, r).start()

    def nb_copy(n, h, s, device):
        return remote(nb.at[h, s], nb.at[h, s], nb_send.at[h, n], nb_recv.at[h, s], device)

    def nb_sends(h):
        to = (across, y_of(1), y_of(3), y_of(2))
        return [nb_copy(n, h, d, at_dp(d_)) for n, d_ in enumerate(to)]

    def nb_forwards(h):
        return [nb_copy(4 + n, h, across, at_dp(y_of(dy))) for n, dy in enumerate((1, 3, 2))]

    def nb_arrived(h, s):
        nb_copy(0, h, s, at_dp(across)).wait_recv()

    def t_nb(h):
        @pl.loop(1, N_G)
        def _(r):
            i, device = peer(r)
            remote(own_f.at[h], stats_f.at[h, i], sf_send.at[h, r], sf_recv.at[h, i], device).wait_recv()

        norm_from(jnp.sum(stats_f[h], axis=0), h)
        normed = (resid[h].astype(F32) - mu[h]) * scale[h] * gain_f[...]
        nb[h, d] = normed.astype(BF16)
        for copy in nb_sends(h):
            copy.start()

    def half_of(k):
        return pick(k, [h for h, r in CHUNKS])

    def replica_of(k):
        return pick(k, [r for h, r in CHUNKS])

    def block(k, a_, z_):
        return up.at[k % RING, c, a_ * 4 + z_]

    def act_block(k, a_, z_):
        return act.at[k, c, a_ * 4 + z_]

    def copy_of(kind, k):
        at = land.at[k]
        src, dst, device = {
            SB: lambda: (up.at[k % RING, oc], sb.at[k], D_S),
            RX1: lambda: (block(k, oa, z2), at.at[L_RX1], D_X),
            RZP: lambda: (block(k, oa, zp), at.at[L_RZP], D_ZP),
            RZM: lambda: (block(k, oa, zm), at.at[L_RZM], D_ZM),
            FX: lambda: (block(k, oa, z), at.at[L_FX], D_X),
            FZP1: lambda: (block(k, a, zp).at[1], at.at[L_FZP, 1], D_ZP),
            FZM0: lambda: (block(k, a, zm).at[0], at.at[L_FZM, 0], D_ZM),
            H0: lambda: (block(k, a, z2).at[0], at.at[L_H, 0], D_ZP),
            H1: lambda: (block(k, a, z2).at[1], at.at[L_H, 1], D_ZM),
            FZP0: lambda: (block(k, a, zp).at[0], at.at[L_FZP, 0], D_ZP),
            FZM1: lambda: (block(k, a, zm).at[1], at.at[L_FZM, 1], D_ZM),
            FZP: lambda: (block(k, a, zp), at.at[L_FZP], D_ZP),
            FZM: lambda: (block(k, a, zm), at.at[L_FZM], D_ZM),
            FZ2: lambda: (block(k, a, z2), at.at[L_H], D_Z2),
            AX: lambda: (act_block(k, a, z),) * 2 + (D_X,),
            AZP: lambda: (act_block(k, a, z),) * 2 + (D_ZP,),
            AZM: lambda: (act_block(k, a, z),) * 2 + (D_ZM,),
            AZ2: lambda: (act_block(k, a, z),) * 2 + (D_Z2,),
            XZP: lambda: (act_block(k, oa, z),) * 2 + (D_ZP,),
            XZM: lambda: (act_block(k, oa, z),) * 2 + (D_ZM,),
            XZ2: lambda: (act_block(k, a, z2),) * 2 + (D_X,),
            ZH0: lambda: (act_block(k, a, zm).at[0],) * 2 + (D_ZP,),
            ZH1: lambda: (act_block(k, a, zp).at[1],) * 2 + (D_ZM,),
            AS: lambda: (act.at[k, c],) * 2 + (D_S,),
        }[kind]()
        return remote(src, dst, send.at[k, kind], recv.at[k, kind], device)

    def got(k, *kinds):
        for kind in kinds:
            if kind < AX:
                copy_of(kind, k).wait_recv()
                continue
            ref = {
                AX: lambda: act_block(k, oa, z),
                AZP: lambda: act_block(k, a, zm),
                AZM: lambda: act_block(k, a, zp),
                AZ2: lambda: act_block(k, a, z2),
                XZP: lambda: act_block(k, oa, zm),
                XZM: lambda: act_block(k, oa, zp),
                XZ2: lambda: act_block(k, oa, z2),
                ZH0: lambda: act_block(k, a, z2).at[0],
                ZH1: lambda: act_block(k, a, z2).at[1],
                AS: lambda: act.at[k, oc],
            }[kind]()
            remote(ref, ref, send.at[k, kind], recv.at[k, kind], D_X).wait_recv()

    def give(k, *kinds):
        for kind in kinds:
            copy_of(kind, k).start()

    def either(condition, yes, no):
        pl.when(condition)(yes)
        pl.when(jnp.logical_not(condition))(no)

    def gave(k, *kinds):
        for kind in kinds:
            copy_of(kind, k).wait_send()

    def sums_sent(k):
        gave(k, SB, RX1, RZP, RZM, FX)
        either(
            k < DIRECT_SUM,
            lambda: gave(k, FZP, FZM, FZ2),
            lambda: gave(k, FZP1, FZM0, H0, H1, FZP0, FZM1),
        )

    def up_product(k):
        h, r = half_of(k), replica_of(k)
        s = ((xh + r // 4) % 2) * 4 + (y + r % 4) % 4
        for n in range(2):

            @pl.when(k == FORWARD_AT[n])
            def _():
                nb_arrived(n, across)
                for copy in nb_forwards(n):
                    copy.start()

        @pl.when(pick(k, [int(r_ not in (0, 4)) for _, r_ in CHUNKS]) == 1)
        def _():
            nb_arrived(h, s)

        @pl.when(k >= RING)
        def _():
            sums_sent(k - RING)

        x = nb[h, s]
        for n in range(4):
            r_ = jnp.dot(x, wu[:, n * 512 : (n + 1) * 512], preferred_element_type=F32)
            up[k % RING, n // 2, :, n % 2] = r_.astype(BF16).reshape(8, 16, 512)
        give(k, SB)

    def pair_sum(k):
        got(k, SB)
        i = k % RING
        up[i, c] = (up[i, c].astype(F32) + sb[k].astype(F32)).astype(BF16)
        give(k, RX1, RZP, RZM)
        either(k < DIRECT_SUM, lambda: give(k, FZP, FZM), lambda: give(k, FZP1, FZM0))

    def second_sum(k):
        i = k % RING
        got(k, RX1)
        b = a * 4 + z2
        up[i, c, b] = (up[i, c, b].astype(F32) + land[k, L_RX1].astype(F32)).astype(BF16)
        either(k < DIRECT_SUM, lambda: give(k, FZ2), lambda: give(k, H0, H1))
        got(k, RZP, RZM)
        b = oa * 4 + z
        both = land[k, L_RZP].astype(F32) + land[k, L_RZM].astype(F32)
        up[i, c, b] = (up[i, c, b].astype(F32) + both).astype(BF16)
        give(k, FX)

    def third_sum(k):
        i = k % RING

        @pl.when(k >= DIRECT_SUM)
        def _():
            for kind, then, z_, half in ((H0, FZP0, zp, 0), (H1, FZM1, zm, 1)):
                got(k, kind)
                b = a * 4 + z_
                both = up[i, c, b, half].astype(F32) + land[k, L_H, half].astype(F32)
                up[i, c, b, half] = both.astype(BF16)
                give(k, then)

    def activate(k):
        i, b = k % RING, a * 4 + z

        def finish(pre, *landings):
            for n in landings:
                pre += land[k, n].astype(F32)
            inner = 0.7978845608028654 * (pre + 0.044715 * (pre * pre * pre))
            act[k, c, b] = (0.5 * pre * (1.0 + jnp.tanh(inner))).astype(BF16)

        def from_four():
            got(k, FZP, FZM, FX, FZ2)
            finish(up[i, c, b].astype(F32), L_FZP, L_FZM, L_FX, L_H)

        def from_three():
            got(k, FZP1, FZM0, FX, FZP0, FZM1)
            finish(up[i, c, b].astype(F32), L_FZP, L_FZM, L_FX)

        either(k < DIRECT_SUM, from_four, from_three)

        @pl.when(k >= DIRECT_GATHER)
        def _():
            give(k, AZ2)

        give(k, AX, AZP, AZM)

    def spread(k):
        got(k, AX)
        give(k, XZP, XZM)

        def direct():
            got(k, AZ2)
            give(k, XZ2)

        def halves():
            got(k, AZP)
            give(k, ZH0)
            got(k, AZM)
            give(k, ZH1)

        either(k >= DIRECT_GATHER, direct, halves)

    def spread_across(k):
        def halves():
            got(k, ZH0, ZH1)
            give(k, XZ2)

        either(k >= DIRECT_GATHER, lambda: got(k, AZP, AZM), halves)

    def down_half(k, c_):
        r = jnp.zeros((HALF, WIDE), F32)
        for q in range(2):
            x = act[k, c_, :, q].reshape(HALF, 512)
            r += jnp.dot(x, wd[c_ * 2 + q], preferred_element_type=F32)
        return r

    def to_sibling(k):
        got(k, XZP, XZM, XZ2)
        give(k, AS)
        part_down[...] = down_half(k, c)

    def dp_copy(k):
        r = replica_of(k)
        x_ = (xh + pick(k, [int(r_ == 4) for _, r_ in CHUNKS])) % 2
        to = at_dp(x_ * 4 + (y + r % 4) % 4)
        return remote(down.at[k], fin.at[half_of(k), r], dp_send.at[k], dp_recv.at[half_of(k), r], to)

    def fin_arrived(h, r):
        remote(down.at[0], fin.at[h, r], dp_send.at[0], dp_recv.at[h, r], at_dp(across)).wait_recv()

    def is_sent(k):
        return pick(k, [int(r_ != 0) for _, r_ in CHUNKS]) == 1

    def down_product(k):
        got(k, AS)
        down[k] = (part_down[...] + down_half(k, oc)).astype(BF16)
        for h in range(2):

            @pl.when(k == CHUNK_OF[h, 4])
            def _():
                total = down[k].astype(F32)
                for r in (5, 6, 7):
                    fin_arrived(h, r)
                    total += fin[h, r].astype(F32)
                down[k] = total.astype(BF16)

        @pl.when(is_sent(k))
        def _():
            dp_copy(k).start()

    tasks = {name[2:]: f for name, f in locals().items() if name.startswith("t_")}
    for name, h in (
        ("s", 0), ("z2", 0), ("x", 0), ("zz", 0), ("x", 1), ("fx", 0), ("z2", 1), ("f2", 0), ("fz", 0),
        ("norm", 0), ("px", 0), ("qz", 0), ("qx", 0), ("q2", 0), ("fx", 1), ("f3", 0), ("p3", 0), ("zz", 1),
        ("f4", 0), ("p0", 0), ("q3", 0), ("p4", 0), ("q4", 0), ("pz", 0), ("p2", 0), ("f2", 1), ("att", 0),
        ("s", 1), ("px", 1), ("opa", 0), ("opb", 0), ("p2", 1), ("f3", 1), ("f4", 1), ("p4", 1), ("q2", 1),
        ("p0", 1), ("fz", 1), ("pz", 1), ("r1", 0), ("r1b", 0), ("q3", 1), ("qx", 1), ("qz", 1), ("q4", 1),
        ("p3", 1), ("att", 1), ("opa", 1), ("r3", 0), ("opb", 1), ("nb", 0),
    ):
        tasks[name](h)
    loads[8].wait()
    loads[9].wait()
    up_product(0)
    t_r1(1)
    t_r1b(1)

    @pl.loop(0, N_K + 7)
    def _(step):
        pl.when(step == 2)(lambda: t_r3(1))
        pl.when(step == 4)(lambda: t_nb(1))
        for f, lag in (
            (pair_sum, 0), (up_product, -1), (second_sum, 1), (third_sum, 2), (down_product, 7),
            (activate, 3), (to_sibling, 6), (spread, 4), (spread_across, 5),
        ):
            k = step - lag
            pl.when(jnp.logical_and(k >= 0, k < N_K))(lambda f=f, k=k: f(k))

    for h in range(2):
        total = resid[h].astype(F32) + down[CHUNK_OF[h, 0]].astype(F32)
        for r in (1, 2, 3, 4):
            fin_arrived(h, r)
            total += fin[h, r].astype(F32)
        o_ref[h] = total.astype(BF16)

    for copy in sends:
        copy.wait_send()
    for h in range(2):
        for copy in nb_sends(h) + nb_forwards(h):
            copy.wait_send()

    @pl.loop(1, N_G)
    def _(r):
        stat_a(r).wait_send()
        stat_f(0, r).wait_send()
        stat_f(1, r).wait_send()

    @pl.loop(N_K - RING, N_K)
    def _(k):
        sums_sent(k)

    @pl.loop(0, N_K)
    def _(k):
        gave(k, AX, AZP, AZM, XZP, XZM, XZ2, AS)
        either(k >= DIRECT_GATHER, lambda: gave(k, AZ2), lambda: gave(k, ZH0, ZH1))
        pl.when(is_sent(k))(lambda: dp_copy(k).wait_send())


def per_device(
    tokens, segment_ids, gain_attn, w_query, w_key, w_value, w_output, gain_ffn, w_up, w_down
):
    rows, share = tokens.shape
    vmem, hbm = pl.BlockSpec(memory_space=pltpu.VMEM), pl.BlockSpec(memory_space=pl.ANY)
    half = (HALF, share)
    dma = pltpu.SemaphoreType.DMA

    def b(*shape):
        return pltpu.VMEM(shape, BF16)

    def f(*shape):
        return pltpu.VMEM(shape, F32)

    out = pl.pallas_call(
        kernel,
        out_shape=jax.ShapeDtypeStruct((2, *half), BF16),
        in_specs=[hbm] * 10,
        out_specs=vmem,
        scratch_shapes=[
            pltpu.VMEM(segment_ids.shape, jnp.int32), f(N_G, 1, share), f(1, share),
            b(*w_query.shape), b(*w_query.shape), b(*w_query.shape), b(*w_output.shape),
            b(*w_up.shape), b(4, 512, share),
            b(N_G, 2, *half), f(2, HALF, 768), b(2, HALF, 256), b(2, 8, 2, *half), b(8, 2, *half),
            b(7, 2, *half), f(2, 8, HALF), f(2, 8, HALF), f(N_G, 2, 8, HALF), f(2, N_G, 8, HALF),
            f(2, *half), f(2, *half), b(2, *half),
            b(2, N_DP, *half), b(RING, 2, 8, 2, 16, 512), b(N_K, 8, 2, 16, 512), b(N_K, 7, 2, 16, 512),
            b(N_K, 2, 8, 2, 16, 512), f(*half), b(N_K, *half), b(2, N_DP, *half),
            dma((10,)), dma((30,)), dma((N_G, 2)), dma((8, 2)), dma((8, 2)), dma((7, 2)), dma((7, 2)),
            dma((N_G,)), dma((N_G,)), dma((2, N_G)), dma((2, N_G)),
            dma((N_K, KINDS)), dma((N_K, KINDS)), dma((2, 7)), dma((2, N_DP)), dma((N_K,)), dma((2, N_DP)),
        ],
        compiler_params=pltpu.CompilerParams(
            collective_id=0, has_side_effects=True, vmem_limit_bytes=62 << 20
        ),
        name="layer",
    )(
        tokens.reshape(2, *half), segment_ids, gain_attn.reshape(N_G, 1, share),
        gain_ffn.reshape(N_G, 1, share), w_query, w_key, w_value, w_output, w_up,
        w_down.reshape(4, 512, share),
    )
    return out.reshape(rows, share)


def solution(mesh):
    return jax.shard_map(
        per_device,
        mesh=mesh,
        in_specs=(
            P("dp", ("section", "tensor")),
            P("dp", None),
            P(),
            P(None, ("section", "tensor")),
            P(None, ("section", "tensor")),
            P(None, ("section", "tensor")),
            P(("section", "tensor"), None),
            P(),
            P(("section", "tensor"), "dp"),
            P("dp", ("section", "tensor")),
        ),
        out_specs=P("dp", ("section", "tensor")),
        check_vma=False,
    )
```

time: 493 us -> 136 us (0.28)
  waiting for transfers between devices: 424 us -> 0 us
  Pallas kernels: 0 us -> 135 us
  matrix products: 33.5 us -> 0 us
  other arithmetic: 16.6 us -> 0 us
  between operations: 13.6 us -> 0.01 us
    all_gather x3 -> x0, waiting for transfers between devices: 152 us -> none  [the longest x1 54.9 us: per_device(): gathered = lax.all_gather(normed_ffn, 'dp', axis=0, tiled=True)]
    reduce_scatter x2 -> x0, waiting for transfers between devices: 144 us -> none  [the longest x1 74.2 us: per_device(): lax.psum_scatter(partial_down.astype(jnp.bfloat16), 'dp', scatter_dimensi...]
    pallas_call x0 -> x1, Pallas kernels: none -> 135 us  [per_device(): pl.pallas_call(kernel, out_shape=jax.ShapeDtypeStruct((2, *half), BF16),...]
    psum x1 -> x0, waiting for transfers between devices: 128 us -> none  [per_device(): lax.psum(partial_out.astype(jnp.bfloat16), ('section', 'tensor'))]
    dot_general x8 -> x0, matrix products: 33.2 us -> none  [the longest x1 9.99 us: per_device(): jnp.dot(lax.all_gather(activated, ('section', 'tensor'), axis=0, tiled=Tr...]
    reduce_sum x2 -> x0, other arithmetic: 8.11 us -> none  [layer_norm(): mean = jnp.mean(values, axis=-1, keepdims=True)]
    convert_element_type x5 -> x0, other arithmetic: 7.66 us -> none  [the longest x1 2.23 us: per_device(): activated = jax.nn.gelu(pre_act, approximate=True).astype(jnp.bfloat16)]
  transfers between devices with their start and end apart: 6 -> 0, of which waited for: 6 -> 0; matrix products, arithmetic and copies ran while one was open for 0% -> 0% of each run, Pallas kernels for 0% -> 0%
where the time goes in v2:
time: 136 us
  Pallas kernels  135 us (99%)
  local copies, waits for them, and re-layouts  1.67 us (1%)
    pallas_call x1, Pallas kernels, per_device(): pl.pallas_call(kernel, out_shape=jax.ShapeDtypeStruct((2, *half), BF16),...  135 us

profile of v2, /device:TPU:1, one launch (start us, length us, event | category | flops | bytes accessed | tf_op | source)
XLA Modules:
  0.0 136.2 jit_solution(8225238284550543338)
XLA Ops:
  0.0 134.6 %layer.1 = bf16[2,128,512]{2,1,0:T(8,128)(2,1)} custom-call(bf16[2,128,512]{2,1,0:T(8,128)(2,1)} %bitcast.7, s32[1,256]{1,0:T(1,128)} %seg_hbm.1, f32[16,1,512]{2,1,0:T(1,128)} %bitcast.8, f32[16,1,512]{2,1,0:T(1,128)} %bitcast.9, bf16[8192,256]{1,0:T(8,128)(2,1)} %wq_hbm.1, bf16[8192,256]{1,0:T(8,128)(2,1)} %wk_hbm.1, bf16[8192,256]{1,0:T(8,128)(2,1)} %wv_hbm.1, ...), custom_call_target="tpu_custom_call" | custom-call | tf_op jit(solution)/shard_map/layer/pallas_call | solution.py:672
  134.6 1.7 %copy.12 = bf16[256,512]{1,0:T(8,128)(2,1)} copy(bf16[256,512]{1,0:T(8,128)(2,1)} %bitcast.6) | data formatting | bytes 524288

commit v3 on v2

--- a/solution.py
+++ b/solution.py
@@ -29,8 +29,13 @@
     SB, RX1, RZP, RZM, FX, FZP1, FZM0, H0, H1, FZP0, FZM1, FZP, FZM, FZ2,
     AX, AZP, AZM, XZP, XZM, XZ2, AS, ZH0, ZH1, AZ2,
 ) = range(24)
-KINDS = 24
+GROUPS = (
+    (SB,), (RX1,), (RZP, RZM), (FX, FZP1, FZM0, FZP0, FZM1, FZP, FZM, FZ2), (H0,), (H1,),
+    (AX,), (AZP,), (AZM,), (XZP, XZM, XZ2), (AS,), (ZH0, ZH1, AZ2),
+)
+GROUP_OF = {kind: n for n, group in enumerate(GROUPS) for kind in group}
 L_RX1, L_RZP, L_RZM, L_FX, L_FZP, L_FZM, L_H = range(7)
+BLOCKS = 15
 
 
 def remote(src, dst, send_sem, recv_sem, device):
@@ -76,7 +81,7 @@
     tok, acc, ctx, part, sib, red, own_a, own_f, stats_a, stats_f, mu, scale, resid,
     nb, up, sb, land, act, part_down, down, fin,
     w_sem, ag_send, ag_recv, sib_send, sib_recv, red_send, red_recv, sa_send, sa_recv, sf_send, sf_recv,
-    send, recv, nb_send, nb_recv, dp_send, dp_recv,
+    sum_send, act_send, recv, nb_send, nb_recv, dp_send, dp_recv,
 ):
     a = lax.axis_index("section")
     t = lax.axis_index("tensor")
@@ -127,22 +132,22 @@
     loads[0].wait()
     for h in range(2):
         own_a[h] = partial_stats(tok[me, h])
-    stats_a[me] = own_a[...]
+    stats_a[0] = own_a[...]
     pl.semaphore_wait(barrier, N_G - 1 + len(dp_peers))
-
-    sends = []
-
-    def go(copy):
-        copy.start()
-        sends.append(copy)
 
     def stat_a(r):
         i, device = peer(r)
-        return remote(own_a, stats_a.at[me], sa_send.at[r], sa_recv.at[me], device)
+        return remote(own_a, stats_a.at[r], sa_send.at[0], sa_recv.at[0], device)
 
     def stat_f(h, r):
         i, device = peer(r)
-        return remote(own_f.at[h], stats_f.at[h, me], sf_send.at[h, r], sf_recv.at[h, me], device)
+        return remote(own_f.at[h], stats_f.at[h, r], sf_send.at[h], sf_recv.at[h], device)
+
+    def all_of(ref, send_sem, recv_sem):
+        return remote(ref, ref, send_sem, recv_sem, D_X)
+
+    others_a = all_of(stats_a.at[pl.ds(1, N_G - 1)], sa_send.at[0], sa_recv.at[0])
+    others_f = [all_of(stats_f.at[h, pl.ds(1, N_G - 1)], sf_send.at[h], sf_recv.at[h]) for h in range(2)]
 
     @pl.loop(1, N_G)
     def _(r):
@@ -155,12 +160,8 @@
         mu[h] = rows_to_columns(mean, WIDE)
         scale[h] = rows_to_columns(inverse, WIDE)
 
-    ags = []
-
     def ag(s, h, device):
-        n = len(ags)
-        ags.append(remote(tok.at[s, h], tok.at[s, h], ag_send.at[n], ag_recv.at[s, h], device))
-        go(ags[n])
+        remote(tok.at[s, h], tok.at[s, h], ag_send.at[0], ag_recv.at[s, h], device).start()
 
     def arrived(s, h):
         remote(tok.at[s, h], tok.at[s, h], ag_send.at[0], ag_recv.at[s, h], D_X).wait_recv()
@@ -219,11 +220,7 @@
     def t_norm(h):
         if h == 0:
 
-            @pl.loop(1, N_G)
-            def _(r):
-                i, device = peer(r)
-                remote(own_a, stats_a.at[i], sa_send.at[r], sa_recv.at[i], device).wait_recv()
-
+            others_a.wait_recv()
             for n in range(2):
                 norm_from(jnp.sum(stats_a[:, n], axis=0), n)
             acc[...] = jnp.zeros_like(acc)
@@ -300,19 +297,19 @@
         return jnp.dot(ctx[h], wo[:, at], preferred_element_type=F32)
 
     def sib_copy(n, h):
-        return remote(part.at[oc, n, h], sib.at[n, h], sib_send.at[n, h], sib_recv.at[n, h], D_S)
+        return remote(part.at[oc, n, h], sib.at[n, h], sib_send.at[0], sib_recv.at[n, h], D_S)
 
     def t_opa(h):
         if h == 0:
             loads[7].wait()
         for n, (a_, z_) in enumerate(order):
             part[oc, n, h] = term(slot(a_, z_, oc), h).astype(BF16)
-            go(sib_copy(n, h))
+            sib_copy(n, h).start()
 
     red_to = (D_X, D_ZP, D_ZM, D_ZP, D_ZM, D_Z2, D_X)
 
     def red_copy(n, h):
-        return remote(part.at[c, n, h], red.at[n, h], red_send.at[n, h], red_recv.at[n, h], red_to[n])
+        return remote(part.at[c, n, h], red.at[n, h], red_send.at[0], red_recv.at[n, h], red_to[n])
 
     def t_opb(h):
         for n, (a_, z_) in enumerate(order):
@@ -320,7 +317,7 @@
             sib_copy(n, h).wait_recv()
             part[c, n, h] = (mine + sib[n, h].astype(F32)).astype(BF16)
             if n < 5:
-                go(red_copy(n, h))
+                red_copy(n, h).start()
 
     def add_landed(n, h, *landings):
         total = part[c, n, h].astype(F32)
@@ -331,41 +328,37 @@
 
     def t_r1(h):
         part[c, 5, h] = add_landed(5, h, 0).astype(BF16)
-        go(red_copy(5, h))
+        red_copy(5, h).start()
 
     def t_r1b(h):
         part[c, 6, h] = add_landed(6, h, 1, 2).astype(BF16)
-        go(red_copy(6, h))
+        red_copy(6, h).start()
 
     def t_r3(h):
         total = tok[me, h].astype(F32) + add_landed(7, h, 3, 4, 6, 5)
         resid[h] = total.astype(BF16)
         own_f[h] = partial_stats(resid[h])
-        stats_f[h, me] = own_f[h]
+        stats_f[h, 0] = own_f[h]
 
         @pl.loop(1, N_G)
         def _(r):
             stat_f(h, r).start()
 
-    def nb_copy(n, h, s, device):
-        return remote(nb.at[h, s], nb.at[h, s], nb_send.at[h, n], nb_recv.at[h, s], device)
+    def nb_copy(h, s, device):
+        return remote(nb.at[h, s], nb.at[h, s], nb_send.at[h], nb_recv.at[h, s], device)
 
     def nb_sends(h):
         to = (across, y_of(1), y_of(3), y_of(2))
-        return [nb_copy(n, h, d, at_dp(d_)) for n, d_ in enumerate(to)]
+        return [nb_copy(h, d, at_dp(d_)) for d_ in to]
 
     def nb_forwards(h):
-        return [nb_copy(4 + n, h, across, at_dp(y_of(dy))) for n, dy in enumerate((1, 3, 2))]
+        return [nb_copy(h, across, at_dp(y_of(dy))) for dy in (1, 3, 2)]
 
     def nb_arrived(h, s):
-        nb_copy(0, h, s, at_dp(across)).wait_recv()
+        nb_copy(h, s, at_dp(across)).wait_recv()
 
     def t_nb(h):
-        @pl.loop(1, N_G)
-        def _(r):
-            i, device = peer(r)
-            remote(own_f.at[h], stats_f.at[h, i], sf_send.at[h, r], sf_recv.at[h, i], device).wait_recv()
-
+        others_f[h].wait_recv()
         norm_from(jnp.sum(stats_f[h], axis=0), h)
         normed = (resid[h].astype(F32) - mu[h]) * scale[h] * gain_f[...]
         nb[h, d] = normed.astype(BF16)
@@ -412,26 +405,11 @@
             ZH1: lambda: (act_block(k, a, zp).at[1],) * 2 + (D_ZM,),
             AS: lambda: (act.at[k, c],) * 2 + (D_S,),
         }[kind]()
-        return remote(src, dst, send.at[k, kind], recv.at[k, kind], device)
-
-    def got(k, *kinds):
-        for kind in kinds:
-            if kind < AX:
-                copy_of(kind, k).wait_recv()
-                continue
-            ref = {
-                AX: lambda: act_block(k, oa, z),
-                AZP: lambda: act_block(k, a, zm),
-                AZM: lambda: act_block(k, a, zp),
-                AZ2: lambda: act_block(k, a, z2),
-                XZP: lambda: act_block(k, oa, zm),
-                XZM: lambda: act_block(k, oa, zp),
-                XZ2: lambda: act_block(k, oa, z2),
-                ZH0: lambda: act_block(k, a, z2).at[0],
-                ZH1: lambda: act_block(k, a, z2).at[1],
-                AS: lambda: act.at[k, oc],
-            }[kind]()
-            remote(ref, ref, send.at[k, kind], recv.at[k, kind], D_X).wait_recv()
+        sent = sum_send.at[k % RING] if kind < AX else act_send.at[0]
+        return remote(src, dst, sent, recv.at[k % RING, GROUP_OF[kind]], device)
+
+    def got(k, kind, ref):
+        all_of(ref, act_send.at[0], recv.at[k % RING, GROUP_OF[kind]]).wait_recv()
 
     def give(k, *kinds):
         for kind in kinds:
@@ -441,17 +419,9 @@
         pl.when(condition)(yes)
         pl.when(jnp.logical_not(condition))(no)
 
-    def gave(k, *kinds):
-        for kind in kinds:
-            copy_of(kind, k).wait_send()
-
     def sums_sent(k):
-        gave(k, SB, RX1, RZP, RZM, FX)
-        either(
-            k < DIRECT_SUM,
-            lambda: gave(k, FZP, FZM, FZ2),
-            lambda: gave(k, FZP1, FZM0, H0, H1, FZP0, FZM1),
-        )
+        i = k % RING
+        all_of(act.at[pl.ds(0, BLOCKS), 0, 0], sum_send.at[i], recv.at[0, 0]).wait_send()
 
     def up_product(k):
         h, r = half_of(k), replica_of(k)
@@ -479,7 +449,7 @@
         give(k, SB)
 
     def pair_sum(k):
-        got(k, SB)
+        got(k, SB, sb.at[k])
         i = k % RING
         up[i, c] = (up[i, c].astype(F32) + sb[k].astype(F32)).astype(BF16)
         give(k, RX1, RZP, RZM)
@@ -487,11 +457,11 @@
 
     def second_sum(k):
         i = k % RING
-        got(k, RX1)
+        got(k, RX1, land.at[k, L_RX1])
         b = a * 4 + z2
         up[i, c, b] = (up[i, c, b].astype(F32) + land[k, L_RX1].astype(F32)).astype(BF16)
         either(k < DIRECT_SUM, lambda: give(k, FZ2), lambda: give(k, H0, H1))
-        got(k, RZP, RZM)
+        got(k, RZP, land.at[k, pl.ds(L_RZP, 2)])
         b = oa * 4 + z
         both = land[k, L_RZP].astype(F32) + land[k, L_RZM].astype(F32)
         up[i, c, b] = (up[i, c, b].astype(F32) + both).astype(BF16)
@@ -503,7 +473,7 @@
         @pl.when(k >= DIRECT_SUM)
         def _():
             for kind, then, z_, half in ((H0, FZP0, zp, 0), (H1, FZM1, zm, 1)):
-                got(k, kind)
+                got(k, kind, land.at[k, L_H, half])
                 b = a * 4 + z_
                 both = up[i, c, b, half].astype(F32) + land[k, L_H, half].astype(F32)
                 up[i, c, b, half] = both.astype(BF16)
@@ -519,11 +489,11 @@
             act[k, c, b] = (0.5 * pre * (1.0 + jnp.tanh(inner))).astype(BF16)
 
         def from_four():
-            got(k, FZP, FZM, FX, FZ2)
+            got(k, FX, land.at[k, pl.ds(L_FX, 4)])
             finish(up[i, c, b].astype(F32), L_FZP, L_FZM, L_FX, L_H)
 
         def from_three():
-            got(k, FZP1, FZM0, FX, FZP0, FZM1)
+            got(k, FX, land.at[k, pl.ds(L_FX, 3)])
             finish(up[i, c, b].astype(F32), L_FZP, L_FZM, L_FX)
 
         either(k < DIRECT_SUM, from_four, from_three)
@@ -535,27 +505,31 @@
         give(k, AX, AZP, AZM)
 
     def spread(k):
-        got(k, AX)
+        got(k, AX, act_block(k, oa, z))
         give(k, XZP, XZM)
 
         def direct():
-            got(k, AZ2)
+            got(k, AZ2, act_block(k, a, z2))
             give(k, XZ2)
 
         def halves():
-            got(k, AZP)
+            got(k, AZP, act_block(k, a, zm))
             give(k, ZH0)
-            got(k, AZM)
+            got(k, AZM, act_block(k, a, zp))
             give(k, ZH1)
 
         either(k >= DIRECT_GATHER, direct, halves)
 
     def spread_across(k):
         def halves():
-            got(k, ZH0, ZH1)
+            got(k, ZH0, act_block(k, a, z2))
             give(k, XZ2)
 
-        either(k >= DIRECT_GATHER, lambda: got(k, AZP, AZM), halves)
+        def direct():
+            got(k, AZP, act_block(k, a, zm))
+            got(k, AZM, act_block(k, a, zp))
+
+        either(k >= DIRECT_GATHER, direct, halves)
 
     def down_half(k, c_):
         r = jnp.zeros((HALF, WIDE), F32)
@@ -565,7 +539,7 @@
         return r
 
     def to_sibling(k):
-        got(k, XZP, XZM, XZ2)
+        got(k, XZP, act.at[k, c, pl.ds(0, 3)])
         give(k, AS)
         part_down[...] = down_half(k, c)
 
@@ -573,7 +547,7 @@
         r = replica_of(k)
         x_ = (xh + pick(k, [int(r_ == 4) for _, r_ in CHUNKS])) % 2
         to = at_dp(x_ * 4 + (y + r % 4) % 4)
-        return remote(down.at[k], fin.at[half_of(k), r], dp_send.at[k], dp_recv.at[half_of(k), r], to)
+        return remote(down.at[k], fin.at[half_of(k), r], dp_send.at[0], dp_recv.at[half_of(k), r], to)
 
     def fin_arrived(h, r):
         remote(down.at[0], fin.at[h, r], dp_send.at[0], dp_recv.at[h, r], at_dp(across)).wait_recv()
@@ -582,7 +556,7 @@
         return pick(k, [int(r_ != 0) for _, r_ in CHUNKS]) == 1
 
     def down_product(k):
-        got(k, AS)
+        got(k, AS, act.at[k, oc])
         down[k] = (part_down[...] + down_half(k, oc)).astype(BF16)
         for h in range(2):
 
@@ -632,27 +606,19 @@
             total += fin[h, r].astype(F32)
         o_ref[h] = total.astype(BF16)
 
-    for copy in sends:
-        copy.wait_send()
+    others_a.wait_send()
     for h in range(2):
-        for copy in nb_sends(h) + nb_forwards(h):
-            copy.wait_send()
-
-    @pl.loop(1, N_G)
-    def _(r):
-        stat_a(r).wait_send()
-        stat_f(0, r).wait_send()
-        stat_f(1, r).wait_send()
+        others_f[h].wait_send()
+        all_of(nb.at[h, pl.ds(0, 7)], nb_send.at[h], nb_recv.at[0, 0]).wait_send()
+    all_of(tok.at[pl.ds(0, 15)], ag_send.at[0], ag_recv.at[0, 0]).wait_send()
+    all_of(part.at[oc], sib_send.at[0], sib_recv.at[0, 0]).wait_send()
+    all_of(part.at[c, pl.ds(0, 7)], red_send.at[0], red_recv.at[0, 0]).wait_send()
+    all_of(down.at[pl.ds(0, 14)], dp_send.at[0], dp_recv.at[0, 0]).wait_send()
+    all_of(act.at[pl.ds(0, BLOCKS)], act_send.at[0], recv.at[0, 0]).wait_send()
 
     @pl.loop(N_K - RING, N_K)
     def _(k):
         sums_sent(k)
-
-    @pl.loop(0, N_K)
-    def _(k):
-        gave(k, AX, AZP, AZM, XZP, XZM, XZ2, AS)
-        either(k >= DIRECT_GATHER, lambda: gave(k, AZ2), lambda: gave(k, ZH0, ZH1))
-        pl.when(is_sent(k))(lambda: dp_copy(k).wait_send())
 
 
 def per_device(
@@ -683,9 +649,9 @@
             f(2, *half), f(2, *half), b(2, *half),
             b(2, N_DP, *half), b(RING, 2, 8, 2, 16, 512), b(N_K, 8, 2, 16, 512), b(N_K, 7, 2, 16, 512),
             b(N_K, 2, 8, 2, 16, 512), f(*half), b(N_K, *half), b(2, N_DP, *half),
-            dma((10,)), dma((30,)), dma((N_G, 2)), dma((8, 2)), dma((8, 2)), dma((7, 2)), dma((7, 2)),
-            dma((N_G,)), dma((N_G,)), dma((2, N_G)), dma((2, N_G)),
-            dma((N_K, KINDS)), dma((N_K, KINDS)), dma((2, 7)), dma((2, N_DP)), dma((N_K,)), dma((2, N_DP)),
+            dma((10,)), dma((1,)), dma((N_G, 2)), dma((1,)), dma((8, 2)), dma((1,)), dma((7, 2)),
+            dma((1,)), dma((1,)), dma((2,)), dma((2,)),
+            dma((RING,)), dma((1,)), dma((RING, len(GROUPS))), dma((2,)), dma((2, N_DP)), dma((1,)), dma((2, N_DP)),
         ],
         compiler_params=pltpu.CompilerParams(
             collective_id=0, has_side_effects=True, vmem_limit_bytes=62 << 20

time: 136 us -> 129 us (0.949)
  Pallas kernels: 135 us -> 127 us
    pallas_call x1, Pallas kernels: 135 us -> 127 us  [per_device(): pl.pallas_call(kernel, out_shape=jax.ShapeDtypeStruct((2, *half), BF16),...]
where the time goes in v3:
time: 129 us; the launch traced here: 128 us
  Pallas kernels  127 us (98%)
  local copies, waits for them, and re-layouts  1.67 us (1%)
    pallas_call x1, Pallas kernels, per_device(): pl.pallas_call(kernel, out_shape=jax.ShapeDtypeStruct((2, *half), BF16),...  127 us

profile of v3, /device:TPU:1, one launch (start us, length us, event | category | flops | bytes accessed | tf_op | source)
XLA Modules:
  0.0 128.5 jit_solution(6251232375029033864)
XLA Ops:
  0.0 126.8 %layer.1 = bf16[2,128,512]{2,1,0:T(8,128)(2,1)} custom-call(bf16[2,128,512]{2,1,0:T(8,128)(2,1)} %bitcast.7, s32[1,256]{1,0:T(1,128)} %seg_hbm.1, f32[16,1,512]{2,1,0:T(1,128)} %bitcast.8, f32[16,1,512]{2,1,0:T(1,128)} %bitcast.9, bf16[8192,256]{1,0:T(8,128)(2,1)} %wq_hbm.1, bf16[8192,256]{1,0:T(8,128)(2,1)} %wk_hbm.1, bf16[8192,256]{1,0:T(8,128)(2,1)} %wv_hbm.1, ...), custom_call_target="tpu_custom_call" | custom-call | tf_op jit(solution)/shard_map/layer/pallas_call | solution.py:638
  126.8 1.7 %copy.12 = bf16[256,512]{1,0:T(8,128)(2,1)} copy(bf16[256,512]{1,0:T(8,128)(2,1)} %bitcast.6) | data formatting | bytes 524288

commit v4 on v3

--- a/solution.py
+++ b/solution.py
@@ -15,13 +15,13 @@
 WIDE = 512
 
 CHUNKS = (
-    (0, 0), (0, 3), (0, 1), (0, 2), (0, 7), (0, 6), (1, 3), (1, 1),
-    (0, 5), (1, 7), (1, 6), (1, 5), (0, 4), (1, 2), (1, 4), (1, 0),
+    (0, 0), (0, 3), (0, 1), (0, 2), (0, 7), (0, 5), (1, 3), (1, 1),
+    (0, 6), (1, 7), (1, 6), (1, 5), (0, 4), (1, 2), (1, 4), (1, 0),
 )
 N_K = len(CHUNKS)
 CHUNK_OF = {chunk: k for k, chunk in enumerate(CHUNKS)}
 FORWARD_AT = (2, 7)
-DIRECT_SUM = 6
+DIRECT_SUM = (0, 4)
 DIRECT_GATHER = 11
 RING = 8
 
@@ -149,10 +149,6 @@
     others_a = all_of(stats_a.at[pl.ds(1, N_G - 1)], sa_send.at[0], sa_recv.at[0])
     others_f = [all_of(stats_f.at[h, pl.ds(1, N_G - 1)], sf_send.at[h], sf_recv.at[h]) for h in range(2)]
 
-    @pl.loop(1, N_G)
-    def _(r):
-        stat_a(r).start()
-
     def norm_from(total, h):
         mean = total[0:1] / 8192.0
         second = total[1:2] / 8192.0
@@ -216,6 +212,11 @@
     def t_f4(h):
         arrived(s_xz2, h)
         ag(s_xz2, h, D_S)
+
+    def t_stat(h):
+        @pl.loop(1, N_G)
+        def _(r):
+            stat_a(r).start()
 
     def t_norm(h):
         if h == 0:
@@ -423,6 +424,9 @@
         i = k % RING
         all_of(act.at[pl.ds(0, BLOCKS), 0, 0], sum_send.at[i], recv.at[0, 0]).wait_send()
 
+    def sums_direct(k):
+        return jnp.logical_and(k >= DIRECT_SUM[0], k < DIRECT_SUM[1])
+
     def up_product(k):
         h, r = half_of(k), replica_of(k)
         s = ((xh + r // 4) % 2) * 4 + (y + r % 4) % 4
@@ -453,14 +457,14 @@
         i = k % RING
         up[i, c] = (up[i, c].astype(F32) + sb[k].astype(F32)).astype(BF16)
         give(k, RX1, RZP, RZM)
-        either(k < DIRECT_SUM, lambda: give(k, FZP, FZM), lambda: give(k, FZP1, FZM0))
+        either(sums_direct(k), lambda: give(k, FZP, FZM), lambda: give(k, FZP1, FZM0))
 
     def second_sum(k):
         i = k % RING
         got(k, RX1, land.at[k, L_RX1])
         b = a * 4 + z2
         up[i, c, b] = (up[i, c, b].astype(F32) + land[k, L_RX1].astype(F32)).astype(BF16)
-        either(k < DIRECT_SUM, lambda: give(k, FZ2), lambda: give(k, H0, H1))
+        either(sums_direct(k), lambda: give(k, FZ2), lambda: give(k, H0, H1))
         got(k, RZP, land.at[k, pl.ds(L_RZP, 2)])
         b = oa * 4 + z
         both = land[k, L_RZP].astype(F32) + land[k, L_RZM].astype(F32)
@@ -470,7 +474,7 @@
     def third_sum(k):
         i = k % RING
 
-        @pl.when(k >= DIRECT_SUM)
+        @pl.when(jnp.logical_not(sums_direct(k)))
         def _():
             for kind, then, z_, half in ((H0, FZP0, zp, 0), (H1, FZM1, zm, 1)):
                 got(k, kind, land.at[k, L_H, half])
@@ -496,7 +500,7 @@
             got(k, FX, land.at[k, pl.ds(L_FX, 3)])
             finish(up[i, c, b].astype(F32), L_FZP, L_FZM, L_FX)
 
-        either(k < DIRECT_SUM, from_four, from_three)
+        either(sums_direct(k), from_four, from_three)
 
         @pl.when(k >= DIRECT_GATHER)
         def _():
@@ -574,27 +578,27 @@
 
     tasks = {name[2:]: f for name, f in locals().items() if name.startswith("t_")}
     for name, h in (
-        ("s", 0), ("z2", 0), ("x", 0), ("zz", 0), ("x", 1), ("fx", 0), ("z2", 1), ("f2", 0), ("fz", 0),
-        ("norm", 0), ("px", 0), ("qz", 0), ("qx", 0), ("q2", 0), ("fx", 1), ("f3", 0), ("p3", 0), ("zz", 1),
-        ("f4", 0), ("p0", 0), ("q3", 0), ("p4", 0), ("q4", 0), ("pz", 0), ("p2", 0), ("f2", 1), ("att", 0),
-        ("s", 1), ("px", 1), ("opa", 0), ("opb", 0), ("p2", 1), ("f3", 1), ("f4", 1), ("p4", 1), ("q2", 1),
-        ("p0", 1), ("fz", 1), ("pz", 1), ("r1", 0), ("r1b", 0), ("q3", 1), ("qx", 1), ("qz", 1), ("q4", 1),
-        ("p3", 1), ("att", 1), ("opa", 1), ("r3", 0), ("opb", 1), ("nb", 0),
+        ("z2", 0), ("x", 0), ("stat", 0), ("s", 0), ("zz", 0), ("x", 1), ("fx", 0), ("fz", 0), ("f2", 0), ("zz", 1),
+        ("norm", 0), ("p0", 0), ("pz", 0), ("fx", 1), ("px", 1), ("f3", 0), ("p2", 0), ("qz", 0), ("q2", 0),
+        ("p3", 0), ("px", 0), ("qx", 1), ("f4", 0), ("p4", 0), ("q3", 0), ("z2", 1), ("qx", 0), ("fz", 1),
+        ("q4", 0), ("att", 0), ("opa", 0), ("s", 1), ("opb", 0), ("p0", 1), ("f2", 1), ("r1b", 0), ("r1", 0),
+        ("qz", 1), ("f3", 1), ("pz", 1), ("f4", 1), ("p3", 1), ("q2", 1), ("q3", 1), ("p2", 1), ("p4", 1),
+        ("q4", 1), ("att", 1), ("r3", 0), ("opa", 1), ("opb", 1), ("nb", 0),
     ):
         tasks[name](h)
     loads[8].wait()
     loads[9].wait()
     up_product(0)
+    t_r1b(1)
     t_r1(1)
-    t_r1b(1)
 
     @pl.loop(0, N_K + 7)
     def _(step):
         pl.when(step == 2)(lambda: t_r3(1))
         pl.when(step == 4)(lambda: t_nb(1))
         for f, lag in (
-            (pair_sum, 0), (up_product, -1), (second_sum, 1), (third_sum, 2), (down_product, 7),
-            (activate, 3), (to_sibling, 6), (spread, 4), (spread_across, 5),
+            (pair_sum, 0), (up_product, -1), (second_sum, 1), (third_sum, 2), (activate, 3),
+            (down_product, 7), (to_sibling, 6), (spread, 4), (spread_across, 5),
         ):
             k = step - lag
             pl.when(jnp.logical_and(k >= 0, k < N_K))(lambda f=f, k=k: f(k))

time: 129 us -> 125 us (0.969)
  Pallas kernels: 127 us -> 124 us
    pallas_call x1, Pallas kernels: 127 us -> 124 us  [per_device(): pl.pallas_call(kernel, out_shape=jax.ShapeDtypeStruct((2, *half), BF16),...]
where the time goes in v4:
time: 125 us
  Pallas kernels  124 us (99%)
  local copies, waits for them, and re-layouts  1.67 us (1%)
    pallas_call x1, Pallas kernels, per_device(): pl.pallas_call(kernel, out_shape=jax.ShapeDtypeStruct((2, *half), BF16),...  124 us

profile of v4, /device:TPU:1, one launch (start us, length us, event | category | flops | bytes accessed | tf_op | source)
XLA Modules:
  0.0 125.4 jit_solution(14622129653213875797)
XLA Ops:
  0.0 123.7 %layer.1 = bf16[2,128,512]{2,1,0:T(8,128)(2,1)} custom-call(bf16[2,128,512]{2,1,0:T(8,128)(2,1)} %bitcast.7, s32[1,256]{1,0:T(1,128)} %seg_hbm.1, f32[16,1,512]{2,1,0:T(1,128)} %bitcast.8, f32[16,1,512]{2,1,0:T(1,128)} %bitcast.9, bf16[8192,256]{1,0:T(8,128)(2,1)} %wq_hbm.1, bf16[8192,256]{1,0:T(8,128)(2,1)} %wk_hbm.1, bf16[8192,256]{1,0:T(8,128)(2,1)} %wv_hbm.1, ...), custom_call_target="tpu_custom_call" | custom-call | tf_op jit(solution)/shard_map/layer/pallas_call | solution.py:642
  123.7 1.7 %copy.12 = bf16[256,512]{1,0:T(8,128)(2,1)} copy(bf16[256,512]{1,0:T(8,128)(2,1)} %bitcast.6) | data formatting | bytes 524288

commit v5 on v4

--- a/solution.py
+++ b/solution.py
@@ -24,6 +24,7 @@
 DIRECT_SUM = (0, 4)
 DIRECT_GATHER = 11
 RING = 8
+AHEAD = 3
 
 (
     SB, RX1, RZP, RZM, FX, FZP1, FZM0, H0, H1, FZP0, FZM1, FZP, FZM, FZ2,
@@ -300,12 +301,16 @@
     def sib_copy(n, h):
         return remote(part.at[oc, n, h], sib.at[n, h], sib_send.at[0], sib_recv.at[n, h], D_S)
 
+    def to_core(n, h):
+        a_, z_ = order[n]
+        part[oc, n, h] = term(slot(a_, z_, oc), h).astype(BF16)
+        sib_copy(n, h).start()
+
     def t_opa(h):
         if h == 0:
             loads[7].wait()
-        for n, (a_, z_) in enumerate(order):
-            part[oc, n, h] = term(slot(a_, z_, oc), h).astype(BF16)
-            sib_copy(n, h).start()
+        for n in range(AHEAD):
+            to_core(n, h)
 
     red_to = (D_X, D_ZP, D_ZM, D_ZP, D_ZM, D_Z2, D_X)
 
@@ -314,6 +319,8 @@
 
     def t_opb(h):
         for n, (a_, z_) in enumerate(order):
+            if n + AHEAD < len(order):
+                to_core(n + AHEAD, h)
             mine = term(slot(a_, z_, c), h)
             sib_copy(n, h).wait_recv()
             part[c, n, h] = (mine + sib[n, h].astype(F32)).astype(BF16)

time: 125 us -> 128 us (1.024)
  Pallas kernels: 124 us -> 126 us
    pallas_call x1, Pallas kernels: 124 us -> 126 us  [per_device(): pl.pallas_call(kernel, out_shape=jax.ShapeDtypeStruct((2, *half), BF16),...]
where the time goes in v5:
time: 128 us
  Pallas kernels  126 us (98%)
  local copies, waits for them, and re-layouts  1.67 us (1%)
    pallas_call x1, Pallas kernels, per_device(): pl.pallas_call(kernel, out_shape=jax.ShapeDtypeStruct((2, *half), BF16),...  126 us

profile of v5, /device:TPU:1, one launch (start us, length us, event | category | flops | bytes accessed | tf_op | source)
XLA Modules:
  0.0 127.9 jit_solution(1280654214300246126)
XLA Ops:
  0.0 126.3 %layer.1 = bf16[2,128,512]{2,1,0:T(8,128)(2,1)} custom-call(bf16[2,128,512]{2,1,0:T(8,128)(2,1)} %bitcast.7, s32[1,256]{1,0:T(1,128)} %seg_hbm.1, f32[16,1,512]{2,1,0:T(1,128)} %bitcast.8, f32[16,1,512]{2,1,0:T(1,128)} %bitcast.9, bf16[8192,256]{1,0:T(8,128)(2,1)} %wq_hbm.1, bf16[8192,256]{1,0:T(8,128)(2,1)} %wk_hbm.1, bf16[8192,256]{1,0:T(8,128)(2,1)} %wv_hbm.1, ...), custom_call_target="tpu_custom_call" | custom-call | tf_op jit(solution)/shard_map/layer/pallas_call | solution.py:649
  126.3 1.7 %copy.12 = bf16[256,512]{1,0:T(8,128)(2,1)} copy(bf16[256,512]{1,0:T(8,128)(2,1)} %bitcast.6) | data formatting | bytes 524288
